TPU v7x, 256 devices: a whole 4x4x8 slice. The times are simulated.
256 devices in a mesh: row: 64 (over x, z, core), col: 4 (over y).
Axes of the slice: x: 4, y: 4, z: 8, core: 2. Of those that a mesh axis runs over, the one named last changes fastest.
Arguments:
- margin: bfloat16 [24576, 24576], P('row', 'col'), may hold values from -0.109375 to 0.109375
- margin_pattern: int32 [96, 96], replicated, may hold values from 0 to 1, as said below
- orbitals_a: bfloat16 [24576, 512], P(('row', 'col')), may hold values from -6 to 6
- pattern_a: int32 [96, 2], replicated, may hold values 0 or 1
- orbitals_b: bfloat16 [24576, 512], P(('col', 'row')), may hold values from -6 to 6
- pattern_b: int32 [96, 2], replicated, may hold values 0 or 1
Outputs:
- induced_a: bfloat16 [24576, 512], P(('row', 'col'))
- induced_b: bfloat16 [24576, 512], P(('col', 'row'))
- orbital_margin: float32 [512, 512], replicated
Inputs may be any that keep to these rules, and one draw needn't show every extreme that they name: margin_pattern[i, j] is 1 where block i of A and block j of B lie near each other in space, else 0.
All inputs are finite; a program needn't handle non-finite values.
Results may differ from a plain program's by a relative error of at most 0.0063.
Values may be sent and summed in bfloat16 or wider, within the bound.
A program may use at most 128 MiB of HBM per device.

v0:
```python
import math

import jax
import jax.numpy as jnp
from jax import lax
from jax.sharding import PartitionSpec as P

BLK = 256


def block_mask(pattern, row_start, row_count, col_start, col_count):
    row_blocks = (row_start + jnp.arange(row_count, dtype=jnp.int32)) // BLK
    col_blocks = (col_start + jnp.arange(col_count, dtype=jnp.int32)) // BLK
    row_onehot = (
        row_blocks[:, None] == jnp.arange(pattern.shape[0], dtype=jnp.int32)[None, :]
    ).astype(jnp.bfloat16)
    col_onehot = (
        col_blocks[:, None] == jnp.arange(pattern.shape[1], dtype=jnp.int32)[None, :]
    ).astype(jnp.bfloat16)
    picked = jnp.dot(
        row_onehot, pattern.astype(jnp.bfloat16), preferred_element_type=jnp.float32
    ).astype(jnp.bfloat16)
    return jnp.einsum("rk,ck->rc", picked, col_onehot, preferred_element_type=jnp.float32).astype(
        jnp.bfloat16
    )


def local(margin, margin_pattern, orbitals_a, pattern_a, orbitals_b, pattern_b):
    row_total = lax.axis_size("row")
    col_total = lax.axis_size("col")
    row_index = lax.axis_index("row")
    col_index = lax.axis_index("col")
    local_rows, local_cols = margin.shape
    orbital_rows, occupied = orbitals_a.shape
    masked_margin = margin * block_mask(
        margin_pattern, row_index * local_rows, local_rows, col_index * local_cols, local_cols
    )
    masked_a = orbitals_a * block_mask(
        pattern_a, (row_index * col_total + col_index) * orbital_rows, orbital_rows, 0, occupied
    )
    masked_b = orbitals_b * block_mask(
        pattern_b, (col_index * row_total + row_index) * orbital_rows, orbital_rows, 0, occupied
    )
    columns = masked_margin
    b_terms = jnp.dot(
        columns,
        lax.all_gather(masked_b, "row", axis=0, tiled=True),
        preferred_element_type=jnp.float32,
    )
    b_image = lax.psum_scatter(b_terms, "col", scatter_dimension=0, tiled=True).astype(jnp.bfloat16)
    orbital_local = jnp.einsum("ki,kj->ij", masked_a, b_image, preferred_element_type=jnp.float32)
    orbital_margin = lax.psum(orbital_local, ("row", "col")) * (
        1.0 / math.sqrt(local_rows * row_total)
    )
    rounded = orbital_margin.astype(jnp.bfloat16)
    factor = 1.0 / math.sqrt(occupied)
    induced_a = (
        jnp.einsum("ik,jk->ij", b_image, rounded, preferred_element_type=jnp.float32) * factor
    ).astype(jnp.bfloat16)
    a_block = lax.all_gather(masked_a, "col", axis=0, tiled=True)
    columns = masked_margin
    a_sum = lax.psum_scatter(
        jnp.einsum("ki,kj->ij", columns, a_block, preferred_element_type=jnp.float32),
        "row",
        scatter_dimension=0,
        tiled=True,
    )
    a_image = a_sum.astype(jnp.bfloat16)
    induced_b = (jnp.dot(a_image, rounded, preferred_element_type=jnp.float32) * factor).astype(
        jnp.bfloat16
    )
    return (induced_a, induced_b, orbital_margin)


def solution(mesh):
    in_specs = (P("row", "col"), P(), P(("row", "col"), None), P(), P(("col", "row"), None), P())
    out_specs = (P(("row", "col"), None), P(("col", "row"), None), P())
    return jax.shard_map(local, mesh=mesh, in_specs=in_specs, out_specs=out_specs, check_vma=False)
```

profile of v0, /device:TPU:1, one launch (start us, length us, event | category | flops | bytes accessed | tf_op | source)
XLA Modules:
  0.0 555.8 jit_solution(2716432044335944448)
XLA Ops:
  7.2 0.0 all-gather.2.cloned.1.call-start
  7.3 1.9 fusion.4
  9.1 0.0 all-gather.2.cloned.1.call-update
  9.2 0.0 reduce-scatter.3.cloned.1.call-start
  9.3 5.1 fusion
  14.4 0.0 copy-start.2
  14.4 0.0 copy-start.3
  14.4 82.3 %all-gather.2.cloned.1.call-done = bf16[6144,512]{1,0:T(8,128)(2,1)} async-done(((bf16[96,512]{1,0:T(8,128)(2,1)}), bf16[6144,512]{1,0:T(8,128)(2,1)}) %all-gather.2.cloned.1.call-update) | async-done | bytes 6291472 | tf_op jit(solution)/shard_map/all_gather | solution.py:47
  96.6 7.7 %fusion.35 = f32[384,512]{1,0:T(8,128)} fusion(bf16[384,6144]{1,0:T(8,128)(2,1)} %fusion, bf16[6144,512]{1,0:T(8,128)(2,1)} %all-gather.2.cloned.1.call-done), kind=kOutput, calls=%fused_computation.67 | convolution fusion | flops 2415919104 | bytes 11796480 | tf_op jit(solution)/shard_map/dot_general | solution.py:45
  104.3 0.0 reduce-scatter.3.cloned.1.call-update
  104.4 0.0 all-reduce.2.cloned.1.call-start
  104.4 0.0 copy-done.2
  104.5 0.0 copy-done.3
  104.5 0.3 fusion.5
  104.8 11.2 %all_gather.7 = bf16[384,512]{1,0:T(8,128)(2,1)S(1)} all-gather(bf16[96,512]{1,0:T(8,128)(2,1)S(1)} %fusion.5), channel_id=1, replica_groups=mesh['row'=64,'col'=4] {'col'}, dimensions={0}, use_global_device_ids=true | all-gather | bytes 491520 | tf_op jit(solution)/shard_map/all_gather | solution.py:60
  116.0 9.3 %reduce-scatter.3.cloned.1.call-done = f32[96,512]{1,0:T(8,128)} async-done(((f32[384,512]{1,0:T(8,128)}), f32[96,512]{1,0:T(8,128)}) %reduce-scatter.3.cloned.1.call-update) | async-done | bytes 196624 | tf_op jit(solution)/shard_map/reduce_scatter | solution.py:50
  125.3 2.2 fusion.14
  127.5 0.0 all-reduce.2.cloned.1.call-update
  127.5 0.0 reduce-scatter.5.cloned.1.call-start
  127.6 8.9 %fusion.36 = f32[6144,512]{1,0:T(8,128)} fusion(bf16[384,6144]{1,0:T(8,128)(2,1)} %fusion, bf16[384,512]{1,0:T(8,128)(2,1)S(1)} %all_gather.7), kind=kOutput, calls=%fused_computation.68 | convolution fusion | flops 2415919104 | bytes 17694720 | tf_op jit(solution)/shard_map/ki,kj->ij/dot_general | solution.py:63
  136.5 0.0 copy-start.1
  136.5 0.0 reduce-scatter.5.cloned.1.call-update
  136.5 249.4 %all-reduce.2.cloned.1.call-done = f32[512,512]{1,0:T(8,128)} async-done(((f32[512,512]{1,0:T(8,128)}), f32[512,512]{1,0:T(8,128)}) %all-reduce.2.cloned.1.call-update) | async-done | bytes 1048592 | tf_op jit(solution)/shard_map/psum | solution.py:52
  385.9 1.3 broadcast_multiply_fusion
  387.3 0.0 copy-done.1
  387.3 0.0 copy-start
  387.3 1.0 fusion.2
  388.3 159.2 %reduce-scatter.5.cloned.1.call-done = f32[96,512]{1,0:T(8,128)} async-done(((f32[6144,512]{1,0:T(8,128)}), f32[96,512]{1,0:T(8,128)}) %reduce-scatter.5.cloned.1.call-update) | async-done | bytes 196624 | tf_op jit(solution)/shard_map/reduce_scatter | solution.py:62
  547.5 1.8 fusion.3
  549.2 0.0 copy-done
  (5 shorter events, 0.1 us)
Async XLA Ops:
  7.2 89.5 %all-gather.2.cloned.1.call-start = ((), (), s32[]{:S(2)}) async-start(), calls=%async_computation.2 | async-start | bytes 6389760 | tf_op jit(solution)/shard_map/all_gather | solution.py:47
  9.2 116.1 %reduce-scatter.3.cloned.1.call-start = ((), (), s32[]{:S(2)}) async-start(), calls=%async_computation.3 | async-start | bytes 983040 | tf_op jit(solution)/shard_map/reduce_scatter | solution.py:50
  14.4 90.1 %copy-start.2 = (bf16[96,512]{1,0:T(8,128)(2,1)S(1)}, bf16[96,512]{1,0:T(8,128)(2,1)}, u32[]{:S(2)}) copy-start(bf16[96,512]{1,0:T(8,128)(2,1)} %param.8) | copy-start | bytes 294916
  14.4 90.1 %copy-start.3 = (s32[96,2]{0,1:T(2,128)S(1)}, s32[96,2]{0,1:T(2,128)}, u32[]{:S(2)}) copy-start(s32[96,2]{0,1:T(2,128)} %param.9) | copy-start | bytes 2308
  104.4 281.6 %all-reduce.2.cloned.1.call-start = ((), (), s32[]{:S(2)}) async-start(), calls=%async_computation.4 | async-start | bytes 2097152 | tf_op jit(solution)/shard_map/psum | solution.py:52
  127.5 419.9 %reduce-scatter.5.cloned.1.call-start = ((), (), s32[]{:S(2)}) async-start(), calls=%async_computation.5 | async-start | bytes 12779520 | tf_op jit(solution)/shard_map/reduce_scatter | solution.py:62
  136.5 250.8 %copy-start.1 = (f32[96,512]{1,0:T(8,128)S(1)}, f32[96,512]{1,0:T(8,128)}, u32[]{:S(2)}) copy-start(f32[96,512]{1,0:T(8,128)} %reduce-scatter.3.cloned.1.call-done) | copy-start | bytes 589828
  387.3 162.0 %copy-start = (f32[512,512]{1,0:T(8,128)}, f32[512,512]{1,0:T(8,128)S(1)}, u32[]{:S(2)}) copy-start(f32[512,512]{1,0:T(8,128)S(1)} %broadcast_multiply_fusion) | copy-start | bytes 3145732
Sparse Core Ops, SparseCore 0:
  11.3 85.2 all-gather.1
  104.5 20.7 reduce-scatter.2
  131.3 254.6 all-reduce.1
  390.7 156.7 reduce-scatter.4
where the time goes:
time: 559 us; the launch traced here: 556 us
  waiting for transfers between devices  500 us (89%)
  matrix products  28.9 us (5%)
  between operations  13.9 us (2%)
  blocking collectives  11.2 us (2%)
    psum x1, waiting for transfers between devices, local(): lax.psum(orbital_local, ('row', 'col'))  249 us
    reduce_scatter x1, waiting for transfers between devices, local(): lax.psum_scatter(jnp.einsum('ki,kj->ij', columns, a_block, preferred_elem...  159 us
    all_gather x1, waiting for transfers between devices, local(): lax.all_gather(masked_b, 'row', axis=0, tiled=True)  82.3 us
    all_gather x1, blocking collectives, local(): a_block = lax.all_gather(masked_a, 'col', axis=0, tiled=True)  11.2 us
  transfers between devices with their start and end apart: 4, of which 4 were waited for; matrix products, arithmetic and copies ran while one was open for 3% of the time, Pallas kernels for 0%

commit v1 on v0

v1 whole, which is shorter than its diff:
```python
import math

import jax
import jax.numpy as jnp
from jax import lax
from jax.experimental import pallas as pl
from jax.experimental.pallas import tpu as pltpu
from jax.sharding import PartitionSpec as P

MESH = pl.DeviceIdType.MESH
F32 = jnp.float32
BF16 = jnp.bfloat16
BLK = 256
NX, NY, NZ = 4, 4, 8
CH = NX * NZ
LEN = ((4, 3), (4, 3), (3, 4), (3, 4), (4, 3))


def up(v, n):
    return lax.rem(v, n)


def contract0(a, b):
    return lax.dot_general(a, b, (((0,), (0,)), ((), ())), preferred_element_type=F32)


def kernel(
    m_ref, pm_ref, a_ref, pa_ref, b_ref, pb_ref,
    oa_ref, ob_ref, oo_ref,
    mbuf, afull, bbuf, bst, terms, zbuf, ubuf, xbuf, bacc, bpart, bslots,
    of32, obf, ar1, s2, ar2, ar3, rbuf, aimg, aother,
    lsem, msend, mrecv, asend, arecv, wsend, wrecv, gsend, grecv,
    rsend, zrecv, urecv, xrecv, bsend, brecv, osend1, orecv1, osend2, orecv2,
    osend3, orecv3, osend4, orecv4, dsend, drecv, ssend, srecv,
):
    r = lax.axis_index("row")
    y = lax.axis_index("col")
    x, z, c = r // (2 * NZ), (r // 2) % NZ, r % 2
    p = x * NZ + z

    def dev(dx, dz, dy, oc=None):
        core = c if oc is None else oc
        return (up(x + dx, NX) * (2 * NZ) + up(z + dz + NZ, NZ) * 2 + core, up(y + dy, NY))

    def chip(k, dz):
        return up(x + k, NX) * NZ + up(z + dz + NZ, NZ)

    def send(src, dst, ssem, rsem, to):
        pltpu.make_async_remote_copy(
            src_ref=src, dst_ref=dst, send_sem=ssem, recv_sem=rsem, device_id=to, device_id_type=MESH
        ).start()

    def got(dst, sem):
        pltpu.make_async_copy(dst, dst, sem).wait()

    other = 1 - c
    sib = dev(0, 0, 0, other)
    own_m = mbuf.at[pl.ds(pl.multiple_of(c * 384, 128), 384)]
    local = pltpu.make_async_copy(m_ref, own_m, lsem)
    local.start()

    def masked(ref, pat, d):
        first, last = (96 * d) // BLK, (96 * d + 95) // BLK
        rows = 96 * d + lax.broadcasted_iota(jnp.int32, (96, BLK), 0)
        inside = rows < (first + 1) * BLK
        parts = []
        for k in range(2):
            keep = jnp.where(inside, pat[first, k].astype(F32), pat[last, k].astype(F32))
            parts.append((ref[:, k * BLK:(k + 1) * BLK].astype(F32) * keep).astype(BF16))
        return parts

    arow = pl.multiple_of(384 * c + 96 * y, 16)
    a0, a1 = masked(a_ref, pa_ref, 4 * r + y)
    afull[pl.ds(arow, 96), 0:256] = a0
    afull[pl.ds(arow, 96), 256:512] = a1
    b0, b1 = masked(b_ref, pb_ref, 64 * y + r)
    here = jnp.where(c == 0, b0.astype(F32), b1.astype(F32)).astype(BF16)
    there = jnp.where(c == 0, b1.astype(F32), b0.astype(F32)).astype(BF16)
    brow = pl.multiple_of(96 * c, 16)
    for h in range(2):
        bbuf[h * CH + p, pl.ds(brow, 96), :] = here[:, h * 128:(h + 1) * 128]
        bst[h, :, :] = there[:, h * 128:(h + 1) * 128]

    partners = [sib]
    for dx in range(NX):
        for dy in range(NY):
            if dx or dy:
                partners.append(dev(dx, 0, dy))
    for dz in range(1, NZ):
        partners.append(dev(0, dz, 0))
    for dy in range(1, NY):
        partners.append(dev(0, 0, dy, other))
    bar = pltpu.get_barrier_semaphore()
    for to in partners:
        pl.semaphore_signal(bar, inc=1, device_id=to, device_id_type=MESH)
    pl.semaphore_wait(bar, len(partners))

    for h in range(2):
        piece = bbuf.at[h * CH + p, pl.ds(brow, 96)]
        send(bst.at[h], piece, wsend, wrecv.at[h], sib)
    own_a = afull.at[pl.ds(arow, 96)]
    for dy in range(NY):
        for oc in range(2):
            if dy or oc:
                to = dev(0, 0, dy, c if oc == 0 else other)
                send(own_a, own_a, asend, arecv.at[2 * dy + oc], to)
    send(m_ref, own_m, msend, mrecv, sib)

    def chunk(h, idx):
        return bbuf.at[h * CH + idx]

    def gsend_to(h, idx, to):
        send(chunk(h, idx), chunk(h, idx), gsend, grecv.at[h * CH + idx], to)

    def gwait(h, idx):
        got(chunk(h, idx), grecv.at[h * CH + idx])

    brow2 = pl.multiple_of(96 * other, 16)
    for h in range(2):
        got(bbuf.at[h * CH + p, pl.ds(brow2, 96)], wrecv.at[h])
    zup, zdown = dev(0, 1, 0), dev(0, -1, 0)
    for k in (1, 3, 2):
        gsend_to(0, p, dev(k, 0, 0))
    gsend_to(0, p, zup)
    gsend_to(0, p, zdown)
    gsend_to(1, p, zup)
    gsend_to(1, p, zdown)
    for k in (1, 3, 2):
        gsend_to(1, p, dev(k, 0, 0))
    for k in (1, 3, 2):
        gwait(0, chip(k, 0))
        gsend_to(0, chip(k, 0), zup)
        gsend_to(0, chip(k, 0), zdown)

    def gather_step(s):
        for k in (0, 4, 1, 3, 2):
            h, kk = (1, 0) if k == 4 else (0, k)
            for way, (lim, sign, to) in enumerate(((LEN[k][0], -1, zup), (LEN[k][1], 1, zdown))):
                if s <= lim:
                    idx = chip(kk, sign * s)
                    gwait(h, idx)
                    if s < lim:
                        gsend_to(h, idx, to)
                    if h == 1:
                        for kx in (1, 3, 2):
                            gsend_to(1, idx, dev(kx, 0, 0))

    ccol = pl.multiple_of(c * BLK, BLK)

    def term_body(q, carry):
        cols = pl.ds(pl.multiple_of(q * 384, 128), 384)
        strips = []
        for i in range(3):
            rows = pl.ds(i * BLK, BLK)
            strip = []
            for j in range(3):
                keep = pm_ref[3 * p + i, 24 * y + (3 * q + j) // 2].astype(F32)
                sub = pl.ds(pl.multiple_of(q * 384 + j * 128, 128), 128)
                tile = mbuf[rows, sub] * jnp.full((BLK, 128), keep, F32).astype(BF16)
                mbuf[rows, sub] = tile
                strip.append(tile)
            strips.append(jnp.concatenate(strip, axis=1))
        tile = jnp.concatenate(strips, axis=0)
        res = contract0(tile, afull[:, pl.ds(ccol, BLK)])
        for e in range(2):
            for h in range(2):
                terms[h * CH + 2 * q + e] = res[192 * e:192 * e + 192, 128 * h:128 * h + 128].astype(BF16)
        return carry

    gather_step(1)
    for dy in range(NY):
        for oc in range(2):
            if dy or oc:
                core = c if oc == 0 else other
                row = pl.multiple_of(384 * core + 96 * up(y - dy + NY, NY), 16)
                got(afull.at[pl.ds(row, 96)], arecv.at[2 * dy + oc])
    local.wait()
    got(mbuf.at[pl.ds(pl.multiple_of(other * 384, 128), 384)], mrecv)
    lax.fori_loop(0, 5, term_body, 0)
    gather_step(2)
    lax.fori_loop(5, 11, term_body, 0)
    gather_step(3)
    lax.fori_loop(11, 16, term_body, 0)
    gather_step(4)

    def t_at(h, idx):
        return terms.at[h * CH + idx]

    order = (4, -3, 3, -2, 2, -1, 1, 0)

    def usend(i):
        for k in (1, 3, 2):
            send(t_at(1, chip(k, order[i])), ubuf.at[3 * i + k - 1], rsend, urecv.at[3 * i + k - 1], dev(k, 0, 0))

    def usum(i):
        total = terms[CH + chip(0, order[i])].astype(F32)
        for k in (1, 3, 2):
            got(ubuf.at[3 * i + k - 1], urecv.at[3 * i + k - 1])
            total += ubuf[3 * i + k - 1].astype(F32)
        return total

    def zslot(k, way, s):
        return (2 * k + way) * 4 + s

    def zsend(src, k, way, s):
        send(src, zbuf.at[zslot(k, way, s)], rsend, zrecv.at[zslot(k, way, s)], zup if way == 0 else zdown)

    def scatter_step(s):
        for k in range(4):
            for way in range(2):
                lim = LEN[k][way]
                if s < lim:
                    idx = chip(k, (lim - s) if way == 0 else (s - lim))
                    if s == 0:
                        zsend(t_at(0, idx), k, way, 0)
                    else:
                        slot = zslot(k, way, s - 1)
                        got(zbuf.at[slot], zrecv.at[slot])
                        zbuf[slot] = (zbuf[slot].astype(F32) + terms[idx].astype(F32)).astype(BF16)
                        zsend(zbuf.at[slot], k, way, s)

    def scatter_step1(s):
        for way in range(2):
            lim = LEN[4][way]
            if s < lim:
                off = (lim - s) if way == 0 else (s - lim)
                total = usum(order.index(off))
                if s > 0:
                    slot = zslot(4, way, s - 1)
                    got(zbuf.at[slot], zrecv.at[slot])
                    total += zbuf[slot].astype(F32)
                first = 3 * order.index(off)
                ubuf[first] = total.astype(BF16)
                zsend(ubuf.at[first], 4, way, s)

    def b_body(g, carry):
        cols = pl.ds(pl.multiple_of(g * 768, 128), 768)
        halves = [bbuf[pl.ds(h * CH + 4 * g, 4)].reshape(768, 128) for h in range(2)]
        bacc[...] += jnp.dot(mbuf[:, cols], jnp.concatenate(halves, axis=1), preferred_element_type=F32)
        return carry

    usend(0)
    scatter_step(0)
    usend(1)
    usend(2)
    for i in range(8):
        for k in (1, 3, 2):
            gwait(1, chip(k, order[i]))
    bacc[...] = jnp.zeros_like(bacc)
    lax.fori_loop(0, 4, b_body, 0)
    scatter_step(1)
    usend(3)
    usend(4)
    scatter_step1(0)
    lax.fori_loop(4, 8, b_body, 0)
    bpart[...] = bacc[...].astype(BF16).reshape(2, NY, 96, BLK)
    for dy in range(NY):
        for oc in range(2):
            if dy or oc:
                core = c if oc == 0 else other
                slot = 2 * dy + oc
                send(bpart.at[core, up(y + dy, NY)], bslots.at[slot], bsend, brecv.at[slot], dev(0, 0, dy, core))
    bslots[0] = bpart[c, y]
    orb = contract0(afull[...], bpart[...].reshape(768, BLK)).reshape(16, 32, BLK)
    of32[...] = orb
    obf[...] = orb.astype(BF16)
    for dx in range(NX):
        for dy in range(NY):
            if dx or dy:
                slot = 4 * dx + dy
                send(obf.at[up(x + dx, NX) * 4 + up(y + dy, NY)], ar1.at[slot], osend1, orecv1.at[slot], dev(dx, 0, dy))
    scatter_step(2)
    usend(5)
    usend(6)
    scatter_step1(1)
    total = of32[4 * x + y]
    for slot in range(1, 16):
        got(ar1.at[slot], orecv1.at[slot])
        total += ar1[slot].astype(F32)
    for e in range(8):
        s2[e] = total[8 * (e // 2):8 * (e // 2) + 8, 128 * (e % 2):128 * (e % 2) + 128]
    for dz in range(1, NZ):
        send(s2.at[up(z + dz, NZ)], ar2.at[dz], osend2, orecv2.at[dz], dev(0, dz, 0))
    scatter_step(3)
    usend(7)
    scatter_step1(2)
    total = s2[z]
    for dz in range(1, NZ):
        got(ar2.at[dz], orecv2.at[dz])
        total += ar2[dz]
    ar3[z] = total * (1.0 / math.sqrt(24576))
    for dz in range(1, NZ):
        send(ar3.at[z], ar3.at[z], osend3, orecv3.at[dz], dev(0, dz, 0))
    scatter_step1(3)

    def zlast(k):
        total = terms[CH * (k == 4) + chip(k % 4, 0)].astype(F32) if k < 4 else usum(7)
        for way in range(2):
            slot = zslot(k, way, LEN[k][way] - 1)
            got(zbuf.at[slot], zrecv.at[slot])
            total += zbuf[slot].astype(F32)
        return total

    for k in (1, 3, 2):
        xbuf[k] = zlast(k).astype(BF16)
        send(xbuf.at[k], xbuf.at[3 + k], rsend, xrecv.at[k], dev(k, 0, 0))
    for dz in range(1, NZ):
        src = up(z - dz + NZ, NZ)
        got(ar3.at[src], orecv3.at[dz])
    piece = jnp.concatenate(
        [jnp.concatenate([ar3[2 * g], ar3[2 * g + 1]], axis=1) for g in range(4)], axis=0
    )
    rbuf[c, 4 * x + y] = piece.astype(BF16)
    for dx in range(NX):
        for dy in range(NY):
            if dx or dy:
                slot = 4 * dx + dy
                mine = rbuf.at[c, 4 * x + y]
                send(mine, mine, osend4, orecv4.at[slot], dev(dx, 0, dy))
    half0 = zlast(0)
    half1 = zlast(4)
    parts = [bslots[0].astype(F32), None]
    for dy in range(NY):
        for oc in range(2):
            slot = 2 * dy + oc
            if slot:
                got(bslots.at[slot], brecv.at[slot])
                v = bslots[slot].astype(F32)
                parts[oc] = v if parts[oc] is None else parts[oc] + v
    b_here, b_there = parts[0].astype(BF16), parts[1].astype(BF16)
    for k in (1, 3, 2):
        got(xbuf.at[3 + k], xrecv.at[k])
        half0 += xbuf[3 + k].astype(F32)
    aimg[:, 0:128] = half0.astype(BF16)
    aimg[:, 128:256] = half1.astype(BF16)
    send(aimg.at[pl.ds(brow2, 96)], aother, ssend, srecv, sib)
    for dx in range(NX):
        for dy in range(NY):
            if dx or dy:
                slot = 4 * dx + dy
                idx = up(x - dx + NX, NX) * 4 + up(y - dy + NY, NY)
                got(rbuf.at[c, idx], orecv4.at[slot])
    send(rbuf.at[c], rbuf.at[c], dsend, drecv, sib)
    factor = 1.0 / math.sqrt(512)

    def dot_t(a, b):
        return lax.dot_general(a, b, (((1,), (1,)), ((), ())), preferred_element_type=F32)

    def half_r(h):
        return rbuf[h].reshape(512, BLK)

    res_a = dot_t(b_here, half_r(c))
    got(aother, srecv)
    got(rbuf.at[other], drecv)
    res_a += dot_t(b_there, half_r(other))
    oa_ref[...] = (res_a * factor).astype(BF16)
    mine = aimg[pl.ds(brow, 96), :]
    theirs = aother[...]
    is0 = c == 0
    left = jnp.where(is0, mine.astype(F32), theirs.astype(F32)).astype(BF16)
    right = jnp.where(is0, theirs.astype(F32), mine.astype(F32)).astype(BF16)
    whole = jnp.concatenate([left, right], axis=1)
    for h in range(2):
        ob_ref[:, h * BLK:(h + 1) * BLK] = (
            jnp.dot(whole, half_r(h), preferred_element_type=F32) * factor
        ).astype(BF16)
        oo_ref[:, h * BLK:(h + 1) * BLK] = half_r(h).astype(F32)

    got(bst, wsend)
    got(afull.at[pl.ds(0, 672)], asend)
    pltpu.make_async_copy(m_ref, own_m, msend).wait()
    got(bbuf.at[pl.ds(0, 62)], gsend)
    got(bbuf.at[pl.ds(0, 62)], rsend)
    got(bslots.at[pl.ds(1, 7)], bsend)
    got(obf.at[pl.ds(0, 15)], osend1)
    got(ar2.at[pl.ds(1, 7)], osend2)
    got(ar2.at[pl.ds(1, 7)], osend3)
    got(obf.at[pl.ds(0, 15)], osend4)
    got(rbuf.at[c], dsend)
    got(aother, ssend)


def local(margin, margin_pattern, orbitals_a, pattern_a, orbitals_b, pattern_b):
    vmem, smem, any_ = (pl.BlockSpec(memory_space=s) for s in (pltpu.VMEM, pltpu.SMEM, pl.ANY))
    dma = pltpu.SemaphoreType.DMA

    def buf(*shape, dtype=BF16):
        return pltpu.VMEM(shape, dtype)

    return pl.pallas_call(
        kernel,
        out_shape=(
            jax.ShapeDtypeStruct((96, 512), BF16),
            jax.ShapeDtypeStruct((96, 512), BF16),
            jax.ShapeDtypeStruct((512, 512), F32),
        ),
        in_specs=[any_, smem, vmem, smem, vmem, smem],
        out_specs=(vmem, vmem, vmem),
        scratch_shapes=[
            buf(768, 6144), buf(768, 512), buf(64, 192, 128), buf(2, 96, 128), buf(64, 192, 128),
            buf(40, 192, 128), buf(24, 192, 128), buf(7, 192, 128),
            buf(768, 256, dtype=F32), buf(2, 4, 96, 256), buf(8, 96, 256),
            buf(16, 32, 256, dtype=F32), buf(16, 32, 256), buf(16, 32, 256),
            buf(8, 8, 128, dtype=F32), buf(8, 8, 128, dtype=F32), buf(8, 8, 128, dtype=F32),
            buf(2, 16, 32, 256), buf(192, 256), buf(96, 256),
            dma, dma, dma, dma, dma((8,)), dma, dma((2,)), dma, dma((64,)),
            dma, dma((40,)), dma((24,)), dma((4,)), dma, dma((8,)), dma, dma((16,)), dma, dma((8,)),
            dma, dma((8,)), dma, dma((16,)), dma, dma, dma, dma,
        ],
        compiler_params=pltpu.CompilerParams(
            collective_id=0, has_side_effects=True, vmem_limit_bytes=48 << 20
        ),
        name="exchange",
    )(margin, margin_pattern, orbitals_a, pattern_a, orbitals_b, pattern_b)


def solution(mesh):
    in_specs = (P("row", "col"), P(), P(("row", "col"), None), P(), P(("col", "row"), None), P())
    out_specs = (P(("row", "col"), None), P(("col", "row"), None), P())
    return jax.shard_map(local, mesh=mesh, in_specs=in_specs, out_specs=out_specs, check_vma=False)
```

time: 559 us -> 85 us (0.15)
  waiting for transfers between devices: 500 us -> 0 us
  Pallas kernels: 0 us -> 77.8 us
  matrix products: 28.9 us -> 0 us
  between operations: 13.9 us -> 0.65 us
  blocking collectives: 11.2 us -> 0 us
  local copies, waits for them, and re-layouts: 0.02 us -> 6.38 us
    psum x1 -> x0, waiting for transfers between devices: 249 us -> none  [local(): lax.psum(orbital_local, ('row', 'col'))]
    reduce_scatter x2 -> x0, waiting for transfers between devices: 168 us -> none  [the longest x1 159 us: local(): lax.psum_scatter(jnp.einsum('ki,kj->ij', columns, a_block, preferred_elem...]
    all_gather x1 -> x0, waiting for transfers between devices: 82.3 us -> none  [local(): lax.all_gather(masked_b, 'row', axis=0, tiled=True)]
    pallas_call x0 -> x1, Pallas kernels: none -> 77.8 us  [local(): pl.pallas_call(kernel, out_shape=(jax.ShapeDtypeStruct((96, 512), BF16),...]
    dot_general x8 -> x0, matrix products: 28.9 us -> none  [the longest x1 8.92 us: local(): jnp.einsum('ki,kj->ij', columns, a_block, preferred_element_type=jnp.floa...]
    all_gather x1 -> x0, blocking collectives: 11.2 us -> none  [local(): a_block = lax.all_gather(masked_a, 'col', axis=0, tiled=True)]
    unnamed x8 -> x11, local copies, waits for them, and re-layouts: 0.02 us -> 6.38 us
  transfers between devices with their start and end apart: 4 -> 0, of which waited for: 4 -> 0; matrix products, arithmetic and copies ran while one was open for 3% -> 0% of each run, Pallas kernels for 0% -> 0%
where the time goes in v1:
time: 85 us; the launch traced here: 84.8 us
  Pallas kernels  77.8 us (92%)
  local copies, waits for them, and re-layouts  6.38 us (8%)
    pallas_call x1, Pallas kernels, local(): pl.pallas_call(kernel, out_shape=(jax.ShapeDtypeStruct((96, 512), BF16),...  77.8 us
    unnamed x11, local copies, waits for them, and re-layouts  6.38 us

profile of v1, /device:TPU:1, one launch (start us, length us, event | category | flops | bytes accessed | tf_op | source)
XLA Modules:
  0.0 84.8 jit_solution(1440051501756732012)
XLA Ops:
  0.6 0.8 copy.9.pa_ref
  1.4 0.8 copy.10.pb_ref
  2.2 0.0 copy-start
  2.2 0.9 %copy-done = bf16[96,512]{1,0:T(8,128)(2,1)S(1)} copy-done((bf16[96,512]{1,0:T(8,128)(2,1)S(1)}, bf16[96,512]{1,0:T(8,128)(2,1)}, u32[]{:S(2)}) %copy-start) | copy-done | bytes 98328
  3.1 0.0 copy-start.1
  3.1 0.9 %copy-done.1 = bf16[96,512]{1,0:T(8,128)(2,1)S(1)} copy-done((bf16[96,512]{1,0:T(8,128)(2,1)S(1)}, bf16[96,512]{1,0:T(8,128)(2,1)}, u32[]{:S(2)}) %copy-start.1) | copy-done | bytes 98328
  4.0 0.0 copy-start.2
  4.0 0.8 copy-done.2
  4.8 77.8 %exchange.1 = (bf16[96,512]{1,0:T(8,128)(2,1)S(1)}, bf16[96,512]{1,0:T(8,128)(2,1)S(1)}, f32[512,512]{1,0:T(8,128)S(1)}) custom-call(bf16[384,6144]{1,0:T(8,128)(2,1)} %m_ref.1, s32[96,96]{1,0:T(8,128)S(1)} %copy-done.2, bf16[96,512]{1,0:T(8,128)(2,1)S(1)} %copy-done, s32[96,2]{1,0:T(8,128)S(1)} %copy.9.pa_ref, bf16[96,512]{1,0:T(8,128)(2,1)S(1)} %copy-done.1, ...), custom_call_target="tpu_custom_call" | custom-call | tf_op jit(solution)/shard_map/exchange/pallas_call | solution.py:390
  82.5 0.6 copy.14
  83.2 0.6 copy.15
  83.8 1.0 %copy.16 = f32[512,512]{1,0:T(8,128)} copy(f32[512,512]{1,0:T(8,128)S(1)} %get-tuple-element.8) | data formatting | bytes 2097152
Async XLA Ops:
  2.2 0.9 %copy-start = (bf16[96,512]{1,0:T(8,128)(2,1)S(1)}, bf16[96,512]{1,0:T(8,128)(2,1)}, u32[]{:S(2)}) copy-start(bf16[96,512]{1,0:T(8,128)(2,1)} %a_ref.1) | copy-start | bytes 294916
  3.1 0.9 %copy-start.1 = (bf16[96,512]{1,0:T(8,128)(2,1)S(1)}, bf16[96,512]{1,0:T(8,128)(2,1)}, u32[]{:S(2)}) copy-start(bf16[96,512]{1,0:T(8,128)(2,1)} %b_ref.1) | copy-start | bytes 294916
  4.0 0.8 copy-start.2

commit v2 on v0

v2 whole, which is shorter than its diff:
```python
import math

import jax
import jax.numpy as jnp
from jax import lax
from jax.experimental import pallas as pl
from jax.experimental.pallas import tpu as pltpu
from jax.sharding import PartitionSpec as P

MESH = pl.DeviceIdType.MESH
F32 = jnp.float32
BF16 = jnp.bfloat16
BLK = 256
NX, NY, NZ = 4, 4, 8
CH = NX * NZ
PART = ((0, 160), (160, 224))
LEN = ((4, 3), (4, 3), (3, 4), (3, 4), (4, 3))

ORDER = (
    ("x0", 1), ("x0", 3), ("z1", 0, 1), ("z1", 1, 1), ("x0", 2), ("apass",), ("x1", 0), ("z0", 0, 0, 1),
    ("z0", 0, 1, 1), ("z0", 1, 0, 1), ("z0", 1, 1, 1), ("aturn",), ("x1", -1), ("terms", 0), ("z1", 0, 2),
    ("z1", 1, 2), ("x1", 1), ("z0", 3, 0, 1), ("z0", 2, 1, 1), ("terms", 1), ("z0", 0, 0, 2), ("z0", 0, 1, 2),
    ("z0", 2, 0, 1), ("terms", 2), ("z0", 1, 0, 2), ("z0", 1, 1, 2), ("z0", 3, 1, 1), ("terms", 3), ("z1", 0, 3),
    ("z1", 1, 3), ("x1", -2), ("x1", 2), ("z0", 2, 1, 2), ("z0", 0, 0, 3), ("z0", 0, 1, 3), ("z0", 3, 0, 2),
    ("bpart", 0), ("z0", 1, 1, 3), ("z0", 2, 0, 2), ("z0", 3, 1, 2), ("z0", 1, 0, 3), ("x1", -3), ("z1", 0, 4),
    ("z0", 2, 1, 3), ("r0", 0, 0, 0), ("r0", 0, 1, 0), ("r0", 1, 0, 0), ("r0", 1, 1, 0), ("u", 4), ("x1", 3),
    ("r0", 2, 0, 0), ("r0", 2, 1, 0), ("r0", 3, 0, 0), ("r0", 3, 1, 0), ("z0", 0, 0, 4), ("z0", 1, 0, 4),
    ("z0", 2, 0, 3), ("z0", 3, 0, 3), ("u", -3), ("z0", 2, 1, 4), ("z0", 3, 1, 3), ("bpart", 1), ("r0", 0, 0, 1),
    ("x1", -4), ("u", 3), ("r0", 0, 1, 1), ("r0", 1, 0, 1), ("r0", 1, 1, 1), ("u", -2), ("r0", 2, 0, 1),
    ("r0", 2, 1, 1), ("r0", 3, 0, 1), ("r0", 3, 1, 1), ("upass", 4), ("bpart", 2), ("z0", 3, 1, 4), ("r0", 0, 0, 2),
    ("u", 2), ("bpart", 3), ("orb",), ("r0", 0, 1, 2), ("r0", 1, 0, 2), ("r0", 1, 1, 2), ("r0", 2, 0, 2),
    ("r0", 2, 1, 2), ("r0", 3, 0, 2), ("r0", 3, 1, 2), ("r0", 0, 0, 3), ("r1", 0, 0), ("upass", -3), ("upass", 3),
    ("r0", 1, 0, 3), ("upass", -2), ("upass", 2), ("u", -1), ("r0", 2, 1, 3), ("r0", 3, 1, 3), ("u", 1), ("r1", 1, 0),
    ("orb2",), ("u", 0), ("r1", 0, 1), ("r0x", 1), ("r0x", 2), ("r0x", 3), ("upass", -1), ("upass", 1), ("r1", 1, 1),
    ("upass", 0), ("r1", 0, 2), ("orb4",), ("r1", 1, 2), ("end0",), ("r1", 0, 3), ("orbend",), ("end1",),
)


def up(v, n):
    return lax.rem(v, n)


def contract0(a, b):
    return lax.dot_general(a, b, (((0,), (0,)), ((), ())), preferred_element_type=F32)


def split(v):
    high = v.astype(BF16)
    return high, (v - high.astype(F32)).astype(BF16)


def kernel(
    m_ref, pm_hbm, a_hbm, pa_ref, b_hbm, pb_ref,
    r_out, b_out, a_out,
    mbuf, afull, at, bbuf, bst, terms, zbuf, zbuf1, ubuf, xbuf, bacc, bpart, bslots,
    of32, obf, ar1, az, rbuf, aimg, aother, bwhole, awhole, a_ref, b_ref, pm_ref,
    lsem, insem, msend, mrecv, asend, arecv, wsend, wrecv, gsend, grecv,
    rsend, zrecv, urecv, xrecv, bsend, brecv, osend1, orecv1, osend2, orecv2,
    osend4, orecv4, dsend, drecv, ssend, srecv, outsem,
):
    r = lax.axis_index("row")
    y = lax.axis_index("col")
    x, z, c = r // (2 * NZ), (r // 2) % NZ, r % 2
    p = x * NZ + z

    def dev(dx, dz, dy, oc=None):
        core = c if oc is None else oc
        return (up(x + dx, NX) * (2 * NZ) + up(z + dz + NZ, NZ) * 2 + core, up(y + dy, NY))

    def chip(k, dz):
        return up(x + k, NX) * NZ + up(z + dz + NZ, NZ)

    def send(src, dst, ssem, rsem, to):
        pltpu.make_async_remote_copy(
            src_ref=src, dst_ref=dst, send_sem=ssem, recv_sem=rsem, device_id=to, device_id_type=MESH
        ).start()

    def got(dst, sem):
        pltpu.make_async_copy(dst, dst, sem).wait()

    other = 1 - c
    sib = dev(0, 0, 0, other)
    zup, zdown = dev(0, 1, 0), dev(0, -1, 0)

    partners = [sib, zup, zdown] + [dev(k, 0, 0) for k in (1, 2, 3)] + [dev(0, 0, k) for k in (1, 2, 3)]
    bar = pltpu.get_barrier_semaphore()
    for to in partners:
        pl.semaphore_signal(bar, inc=1, device_id=to, device_id_type=MESH)
    loads = []
    for i, (src, dst) in enumerate(((b_hbm, b_ref), (a_hbm, a_ref), (pm_hbm, pm_ref))):
        loads.append(pltpu.make_async_copy(src, dst, insem.at[i]))
        loads[-1].start()
    own_m = mbuf.at[pl.ds(pl.multiple_of(c * 384, 128), 384)]
    local = pltpu.make_async_copy(m_ref, own_m, lsem)
    local.start()

    def masked(ref, pat, d):
        first, last = (96 * d) // BLK, (96 * d + 95) // BLK
        rows = 96 * d + lax.broadcasted_iota(jnp.int32, (96, BLK), 0)
        inside = rows < (first + 1) * BLK
        parts = []
        for k in range(2):
            keep = jnp.where(inside, pat[k, first].astype(F32), pat[k, last].astype(F32))
            parts.append((ref[:, k * BLK:(k + 1) * BLK].astype(F32) * keep).astype(BF16))
        return parts

    loads[0].wait()
    b0, b1 = masked(b_ref, pb_ref, 64 * y + r)
    here = jnp.where(c == 0, b0.astype(F32), b1.astype(F32)).astype(BF16)
    there = jnp.where(c == 0, b1.astype(F32), b0.astype(F32)).astype(BF16)
    brow = pl.multiple_of(96 * c, 16)
    for h in range(2):
        bbuf[p, pl.ds(pl.multiple_of(192 * h + 96 * c, 16), 96), :] = here[:, h * 128:(h + 1) * 128]
        bst[h, :, :] = there[:, h * 128:(h + 1) * 128]

    loads[1].wait()
    arow = pl.multiple_of(384 * c + 96 * y, 16)
    a0, a1 = masked(a_ref, pa_ref, 4 * r + y)
    afull[pl.ds(arow, 96), 0:256] = a0
    afull[pl.ds(arow, 96), 256:512] = a1
    pl.semaphore_wait(bar, len(partners))

    for h in range(2):
        piece = bbuf.at[p, pl.ds(pl.multiple_of(192 * h + 96 * c, 16), 96)]
        send(bst.at[h], piece, wsend, wrecv.at[h], sib)
    def a_rows(core, dy):
        return afull.at[pl.ds(pl.multiple_of(384 * core + 96 * up(y + NY - dy, NY), 16), 96)]

    own_a = a_rows(c, 0)
    send(own_a, own_a, asend, arecv.at[4], sib)
    for dy in (1, 3, 2):
        send(own_a, own_a, asend, arecv.at[dy], dev(0, 0, dy))

    def margin_piece(i):
        def body(t, carry):
            j = 6 * i + t
            cols = pl.ds(pl.multiple_of(BLK * j, BLK), BLK)
            for e in range(3):
                rows = pl.ds(pl.multiple_of(384 * c + 128 * e, 128), 128)
                keep = pm_ref[3 * p + (3 * c + e) // 2, 24 * y + j].astype(F32)
                mbuf[rows, cols] = mbuf[rows, cols] * jnp.full((128, BLK), keep, F32).astype(BF16)
            return carry

        lax.fori_loop(0, 6, body, 0)
        piece = mbuf.at[pl.ds(pl.multiple_of(384 * c, 128), 384), pl.ds(1536 * i, 1536)]
        send(piece, piece, msend, mrecv.at[i], sib)

    local.wait()
    loads[2].wait()
    margin_piece(0)
    margin_piece(1)

    def chunk(h, idx):
        return bbuf.at[idx, pl.ds(*PART[h])]

    def gsend_to(h, idx, to):
        send(chunk(h, idx), chunk(h, idx), gsend, grecv.at[h * CH + idx], to)

    def gwait(h, idx):
        got(chunk(h, idx), grecv.at[h * CH + idx])

    brow2 = pl.multiple_of(96 * other, 16)
    for h in range(2):
        got(bbuf.at[p, pl.ds(pl.multiple_of(192 * h + 96 * other, 16), 96)], wrecv.at[h])
    for k in (1, 3, 2):
        gsend_to(0, p, dev(k, 0, 0))
    gsend_to(1, p, zup)
    gsend_to(1, p, zdown)
    gsend_to(0, p, zup)
    gsend_to(0, p, zdown)
    for k in (1, 3):
        gsend_to(1, p, dev(k, 0, 0))
    margin_piece(2)
    margin_piece(3)

    def do_x0(k):
        gwait(0, chip(k, 0))
        gsend_to(0, chip(k, 0), zup)
        gsend_to(0, chip(k, 0), zdown)

    def do_z0(k, way, s):
        idx = chip(k, s if way else -s)
        gwait(0, idx)
        if s < LEN[k][way]:
            gsend_to(0, idx, zdown if way else zup)

    def do_z1(way, s):
        idx = chip(0, s if way else -s)
        gwait(1, idx)
        if s < LEN[4][way]:
            gsend_to(1, idx, zdown if way else zup)
        for k in (1, 3):
            gsend_to(1, idx, dev(k, 0, 0))

    def offsets(s):
        return (0,) if s == 0 else (-s, s) if s < 4 else (-s,)

    def do_x1(off):
        odd_chunk = (z + off + NZ) % 2
        gwait(1, chip(1, off))
        gwait(1, chip(3, off))
        gsend_to(1, chip(3 - 2 * odd_chunk, off), dev(1 + 2 * odd_chunk, 0, 0))

    def gather_last(s):
        for off in offsets(s):
            gwait(1, chip(2, off))

    ccol = pl.multiple_of(c * BLK, BLK)

    def term_body(q, carry):
        cols = pl.ds(pl.multiple_of(q * 768, 128), 768)
        both = jnp.dot(at[pl.ds(ccol, BLK), :], mbuf[:, cols], preferred_element_type=F32)
        low_lanes = lax.broadcasted_iota(jnp.int32, (64, 128), 1) < 64
        for u in range(4):
            h, pair = u % 2, u // 2
            whole = both[128 * h:128 * h + 128, 384 * pair:384 * pair + 384]
            top, bottom = whole[0:64, 128:256], whole[64:128, 128:256]
            first = jnp.where(low_lanes, top, pltpu.roll(bottom, 64, 1))
            second = jnp.where(low_lanes, pltpu.roll(top, 64, 1), bottom)
            for e, (tile_e, rest) in enumerate(((whole[:, 0:128], first), (whole[:, 256:384], second))):
                chunk_at = 4 * q + 2 * pair + e
                terms[chunk_at, 192 * h:192 * h + 128, :] = tile_e.astype(BF16)
                terms[chunk_at, 192 * h + 128:192 * h + 192, :] = rest.astype(BF16)
        return carry

    halfz, odd = z // 2, z % 2

    def do_terms(i):
        if i == 0:
            for j in range(4):
                got(mbuf.at[pl.ds(pl.multiple_of(384 * other, 128), 384), pl.ds(1536 * j, 1536)], mrecv.at[j])
        lax.fori_loop(2 * i, 2 * i + 2, term_body, 0)

    def do_bpart(i):
        if i == 0:
            gather_last(0)
        gather_last(i + 1)
        shift = (0, 3 + 2 * odd, 1 + 2 * odd, 2)[i]
        pair = up(halfz + shift, NZ // 2)
        tiles, rows = [], []
        for k in range(NX):
            first = up(x + k, NX) * NZ + 2 * pair
            tiles.append(mbuf[:, pl.ds(pl.multiple_of(192 * first, 128), 384)])
            halves = [bbuf[pl.ds(first, 2), 192 * h:192 * h + 192, :].reshape(384, 128) for h in range(2)]
            rows.append(jnp.concatenate(halves, axis=1))
        part = jnp.dot(
            jnp.concatenate(tiles, axis=1), jnp.concatenate(rows, axis=0), preferred_element_type=F32
        )
        bacc[...] = part if i == 0 else bacc[...] + part

    def do_apass():
        for dy in (1, 3, 2):
            got(a_rows(c, dy), arecv.at[dy])
            send(a_rows(c, dy), a_rows(c, dy), asend, arecv.at[4 + dy], sib)

    def do_aturn():
        for dy in (0, 1, 3, 2):
            got(a_rows(other, dy), arecv.at[4 + dy])
        at[...] = afull[...].T

    def t_at(h, idx):
        return terms.at[idx, pl.ds(*PART[h])]

    def t_val(h, idx):
        return terms[idx, pl.ds(*PART[h]), :].astype(F32)

    order = (4, -3, 3, -2, 2, -1, 1, 0)

    def ways(off):
        odd_chunk = (z + off + NZ) % 2
        return 1 + 2 * odd_chunk, 3 - 2 * odd_chunk

    def do_u(off):
        i = 3 * order.index(off)
        ahead, back = ways(off)
        send(t_at(1, chip(2, off)), ubuf.at[i], rsend, urecv.at[i], dev(ahead, 0, 0))
        send(t_at(1, chip(back, off)), ubuf.at[i + 1], rsend, urecv.at[i + 1], dev(back, 0, 0))

    def do_upass(off):
        i = 3 * order.index(off)
        ahead, _ = ways(off)
        got(ubuf.at[i], urecv.at[i])
        ubuf[i] = (ubuf[i].astype(F32) + t_val(1, chip(ahead, off))).astype(BF16)
        send(ubuf.at[i], ubuf.at[i + 2], rsend, urecv.at[i + 2], dev(ahead, 0, 0))

    def usum(off):
        total = t_val(1, chip(0, off))
        i = 3 * order.index(off)
        for j in (i + 1, i + 2):
            got(ubuf.at[j], urecv.at[j])
            total += ubuf[j].astype(F32)
        return total

    def zref(k, way, s):
        if k == 4:
            return zbuf1.at[4 * way + s], zrecv.at[32 + 4 * way + s]
        slot = 8 * k + 4 * way + s
        return zbuf.at[slot], zrecv.at[slot]

    def zsend(src, k, way, s):
        dst, sem = zref(k, way, s)
        send(src, dst, rsend, sem, zup if way == 0 else zdown)

    def do_r0(k, way, s):
        lim = LEN[k][way]
        idx = chip(k, (s - lim) if way else (lim - s))
        if s == 0:
            zsend(t_at(0, idx), k, way, 0)
        else:
            ref, sem = zref(k, way, s - 1)
            got(ref, sem)
            ref[...] = (ref[...].astype(F32) + t_val(0, idx)).astype(BF16)
            zsend(ref, k, way, s)

    def do_r1(way, s):
        lim = LEN[4][way]
        off = (s - lim) if way else (lim - s)
        total = usum(off)
        if s > 0:
            ref, sem = zref(4, way, s - 1)
            got(ref, sem)
            total += ref[...].astype(F32)
        mine = ubuf.at[3 * order.index(off) + 1]
        mine[...] = total.astype(BF16)
        zsend(mine, 4, way, s)

    def plane():
        return [(4 * dx + dy, dx, dy) for dx in range(NX) for dy in range(NY) if dx or dy]

    def do_orb():
        b_all = bacc[...]
        high = b_all.astype(BF16)
        low = (b_all - high.astype(F32)).astype(BF16)
        bpart[...] = high.reshape(2, NY, 96, BLK)
        orb = jnp.dot(at[...], high, preferred_element_type=F32)
        orb += jnp.dot(at[...], low, preferred_element_type=F32)
        orb = orb.reshape(16, 32, BLK)
        of32[...] = orb
        obf[...] = orb.astype(BF16)
        for slot, dx, dy in plane():
            src = obf.at[up(x + dx, NX) * 4 + up(y + dy, NY)]
            send(src, ar1.at[slot], osend1, orecv1.at[slot], dev(dx, 0, dy))
        for dy in range(NY):
            for oc in range(2):
                if dy or oc:
                    core = c if oc == 0 else other
                    slot = 2 * dy + oc
                    src = bpart.at[core, up(y + dy, NY)]
                    send(src, bslots.at[slot], bsend, brecv.at[slot], dev(0, 0, dy, core))
        bslots[0] = bpart[c, y]

    def do_orb2():
        total = of32[4 * x + y]
        for slot, _, _ in plane():
            got(ar1.at[slot], orecv1.at[slot])
            total += ar1[slot].astype(F32)
        az[z] = total.astype(BF16)
        for dz in (4, 3, 5, 2, 6, 1, 7):
            send(az.at[z], az.at[z], osend2, orecv2.at[dz], dev(0, dz, 0))

    def do_orb4():
        for dz in range(1, NZ):
            got(az.at[up(z - dz + NZ, NZ)], orecv2.at[dz])
        total = az[0].astype(F32)
        for i in range(1, NZ):
            total += az[i].astype(F32)
        mine = rbuf.at[c, 4 * x + y]
        mine[...] = (total * (1.0 / math.sqrt(24576))).astype(BF16)
        for slot, dx, dy in plane():
            send(mine, mine, osend4, orecv4.at[slot], dev(dx, 0, dy))

    def zlast(k):
        total = t_val(0, chip(k, 0)) if k < 4 else usum(0)
        for way in range(2):
            ref, sem = zref(k, way, LEN[k][way] - 1)
            got(ref, sem)
            total += ref[...].astype(F32)
        return total

    def do_r0x(k):
        xbuf[k] = zlast(k).astype(BF16)
        send(xbuf.at[k], xbuf.at[3 + k], rsend, xrecv.at[k], dev(k, 0, 0))

    halves = []

    def do_end0():
        total = zlast(0)
        for k in (1, 3, 2):
            got(xbuf.at[3 + k], xrecv.at[k])
            total += xbuf[3 + k].astype(F32)
        halves.append(total)
        for oc in range(2):
            total = 0.0
            for dy in range(NY):
                slot = 2 * dy + oc
                if slot:
                    got(bslots.at[slot], brecv.at[slot])
                total += bslots[slot].astype(F32)
            bwhole[c if oc == 0 else other] = total
        pltpu.make_async_copy(bwhole, b_out, outsem.at[0]).start()

    def do_end1():
        halves.append(zlast(4))

    def do_orbend():
        for slot, dx, dy in plane():
            got(rbuf.at[c, up(x - dx + NX, NX) * 4 + up(y - dy + NY, NY)], orecv4.at[slot])
        send(rbuf.at[c], rbuf.at[c], dsend, drecv, sib)

    steps = dict(
        x0=do_x0, z0=do_z0, z1=do_z1, x1=do_x1, apass=do_apass, aturn=do_aturn, terms=do_terms, bpart=do_bpart,
        u=do_u, upass=do_upass, r0=do_r0, r1=do_r1, r0x=do_r0x, orb=do_orb, orb2=do_orb2, orb4=do_orb4,
        orbend=do_orbend, end0=do_end0, end1=do_end1,
    )
    for name, *where in ORDER:
        steps[name](*where)

    image = jnp.concatenate(halves, axis=0)
    for h in range(2):
        lanes = pl.ds(128 * h, 128)
        packed = image[192 * h + 128:192 * h + 192, :]
        rest = jnp.concatenate([packed, pltpu.roll(packed, 64, 1)], axis=0).T
        aimg[pl.ds(pl.multiple_of(64 * odd, 8), 128), lanes] = image[192 * h:192 * h + 128, :].T
        aimg[pl.ds(pl.multiple_of(128 * (1 - odd), 8), 64), lanes] = rest[0:64, :]
    send(aimg.at[pl.ds(pl.multiple_of(96 * other, 8), 96)], aother, ssend, srecv, sib)
    got(rbuf.at[other], drecv)
    pltpu.make_async_copy(rbuf, r_out, outsem.at[1]).start()
    awhole[c] = aimg[pl.ds(brow, 96), :]
    got(aother, srecv)
    awhole[other] = aother[...]
    pltpu.make_async_copy(awhole, a_out, outsem.at[2]).start()

    for i, (src, dst) in enumerate(((bwhole, b_out), (rbuf, r_out), (awhole, a_out))):
        pltpu.make_async_copy(src, dst, outsem.at[i]).wait()
    got(bst, wsend)
    got(afull.at[pl.ds(0, 672)], asend)
    got(own_m, msend)
    got(bbuf.at[pl.ds(0, 31)], gsend)
    got(bbuf.at[pl.ds(0, 31)], rsend)
    got(bslots.at[pl.ds(1, 7)], bsend)
    got(obf.at[pl.ds(0, 15)], osend1)
    got(obf.at[pl.ds(0, 7)], osend2)
    got(obf.at[pl.ds(0, 15)], osend4)
    got(rbuf.at[c], dsend)
    got(aother, ssend)


def last_kernel(r_ref, b_ref, a_ref, oa_ref, ob_ref, oo_ref):
    factor = 1.0 / math.sqrt(512)
    res_a, res_b = 0.0, [0.0, 0.0]
    for h in range(2):
        oo_ref[:, h * BLK:(h + 1) * BLK] = r_ref[h].reshape(512, BLK).astype(F32)
    for h in range(2):
        half = r_ref[h].reshape(512, BLK)
        for v in split(b_ref[h]):
            res_a += lax.dot_general(v, half, (((1,), (1,)), ((), ())), preferred_element_type=F32)
        for v in split(a_ref[h]):
            for j in range(2):
                rows = r_ref[j, 8 * h:8 * h + 8].reshape(BLK, BLK)
                res_b[j] += jnp.dot(v, rows, preferred_element_type=F32)
    oa_ref[...] = (res_a * factor).astype(BF16)
    for j in range(2):
        ob_ref[:, j * BLK:(j + 1) * BLK] = (res_b[j] * factor).astype(BF16)


def local(margin, margin_pattern, orbitals_a, pattern_a, orbitals_b, pattern_b):
    vmem, smem, any_ = (pl.BlockSpec(memory_space=s) for s in (pltpu.VMEM, pltpu.SMEM, pl.ANY))
    dma = pltpu.SemaphoreType.DMA

    def buf(*shape, dtype=BF16):
        return pltpu.VMEM(shape, dtype)

    middle = pl.pallas_call(
        kernel,
        out_shape=(
            jax.ShapeDtypeStruct((2, 16, 32, 256), BF16),
            jax.ShapeDtypeStruct((2, 96, 256), F32),
            jax.ShapeDtypeStruct((2, 96, 256), F32),
        ),
        in_specs=[any_, any_, any_, smem, any_, smem],
        out_specs=(any_, any_, any_),
        scratch_shapes=[
            buf(768, 6144), buf(768, 512), buf(512, 768), buf(32, 384, 128), buf(2, 96, 128), buf(32, 384, 128),
            buf(32, 160, 128), buf(8, 224, 128), buf(24, 224, 128), buf(7, 160, 128),
            buf(768, 256, dtype=F32), buf(2, 4, 96, 256), buf(8, 96, 256),
            buf(16, 32, 256, dtype=F32), buf(16, 32, 256), buf(16, 32, 256),
            buf(8, 32, 256), buf(2, 16, 32, 256), buf(192, 256, dtype=F32), buf(96, 256, dtype=F32),
            buf(2, 96, 256, dtype=F32), buf(2, 96, 256, dtype=F32),
            buf(96, 512), buf(96, 512), pltpu.SMEM((96, 96), jnp.int32),
            dma, dma((3,)), dma, dma((4,)), dma, dma((8,)), dma, dma((2,)), dma, dma((64,)),
            dma, dma((40,)), dma((24,)), dma((4,)), dma, dma((8,)), dma, dma((16,)), dma, dma((8,)),
            dma, dma((16,)), dma, dma, dma, dma, dma((3,)),
        ],
        compiler_params=pltpu.CompilerParams(
            collective_id=0, has_side_effects=True, vmem_limit_bytes=60 << 20
        ),
        name="exchange",
    )(margin, margin_pattern, orbitals_a, pattern_a.T, orbitals_b, pattern_b.T)
    return pl.pallas_call(
        last_kernel,
        out_shape=(
            jax.ShapeDtypeStruct((96, 512), BF16),
            jax.ShapeDtypeStruct((96, 512), BF16),
            jax.ShapeDtypeStruct((512, 512), F32),
        ),
        in_specs=[vmem, vmem, vmem],
        out_specs=(vmem, vmem, vmem),
        compiler_params=pltpu.CompilerParams(vmem_limit_bytes=60 << 20),
        name="last",
    )(*middle)


def solution(mesh):
    in_specs = (P("row", "col"), P(), P(("row", "col"), None), P(), P(("col", "row"), None), P())
    out_specs = (P(("row", "col"), None), P(("col", "row"), None), P())
    return jax.shard_map(local, mesh=mesh, in_specs=in_specs, out_specs=out_specs, check_vma=False)
```

time: 559 us -> 67.9 us (0.12)
  waiting for transfers between devices: 500 us -> 0 us
  Pallas kernels: 0 us -> 67.2 us
  matrix products: 28.9 us -> 0 us
  between operations: 13.9 us -> 0.64 us
  blocking collectives: 11.2 us -> 0 us
    psum x1 -> x0, waiting for transfers between devices: 249 us -> none  [local(): lax.psum(orbital_local, ('row', 'col'))]
    reduce_scatter x2 -> x0, waiting for transfers between devices: 168 us -> none  [the longest x1 159 us: local(): lax.psum_scatter(jnp.einsum('ki,kj->ij', columns, a_block, preferred_elem...]
    all_gather x1 -> x0, waiting for transfers between devices: 82.3 us -> none  [local(): lax.all_gather(masked_b, 'row', axis=0, tiled=True)]
    pallas_call x0 -> x2, Pallas kernels: none -> 67.2 us  [the longest x1 64.4 us: local(): pl.pallas_call(kernel, out_shape=(jax.ShapeDtypeStruct((2, 16, 32, 256),...]
    dot_general x8 -> x0, matrix products: 28.9 us -> none  [the longest x1 8.92 us: local(): jnp.einsum('ki,kj->ij', columns, a_block, preferred_element_type=jnp.floa...]
    all_gather x1 -> x0, blocking collectives: 11.2 us -> none  [local(): a_block = lax.all_gather(masked_a, 'col', axis=0, tiled=True)]
  transfers between devices with their start and end apart: 4 -> 0, of which waited for: 4 -> 0; matrix products, arithmetic and copies ran while one was open for 3% -> 0% of each run, Pallas kernels for 0% -> 0%
where the time goes in v2:
time: 67.9 us; the launch traced here: 67.8 us
  Pallas kernels  67.2 us (99%)
    pallas_call x1, Pallas kernels, local(): pl.pallas_call(kernel, out_shape=(jax.ShapeDtypeStruct((2, 16, 32, 256),...  64.4 us
    pallas_call x1, Pallas kernels, local(): pl.pallas_call(last_kernel, out_shape=(jax.ShapeDtypeStruct((96, 512), BF...  2.82 us

profile of v2, /device:TPU:1, one launch (start us, length us, event | category | flops | bytes accessed | tf_op | source)
XLA Modules:
  0.0 67.8 jit_solution(7288768942255897672)
XLA Ops:
  0.6 64.4 %exchange.1 = (bf16[2,16,32,256]{3,2,1,0:T(8,128)(2,1)}, f32[2,96,256]{2,1,0:T(8,128)}, f32[2,96,256]{2,1,0:T(8,128)}) custom-call(bf16[384,6144]{1,0:T(8,128)(2,1)} %m_ref.1, s32[96,96]{1,0:T(8,128)} %pm_hbm.1, bf16[96,512]{1,0:T(8,128)(2,1)} %a_hbm.1, s32[2,96]{1,0:T(2,128)} %bitcast.2, bf16[96,512]{1,0:T(8,128)(2,1)} %b_hbm.1, s32[2,96]{1,0:T(2,128)} %bitcast.3), custom_call_target="tpu_custom_call" | custom-call | tf_op jit(solution)/shard_map/exchange/pallas_call | solution.py:473
  65.0 2.8 %last.1 = (bf16[96,512]{1,0:T(8,128)(2,1)}, bf16[96,512]{1,0:T(8,128)(2,1)}, f32[512,512]{1,0:T(8,128)}) custom-call(bf16[2,16,32,256]{3,2,1,0:T(8,128)(2,1)} %get-tuple-element.6.r_ref, f32[2,96,256]{2,1,0:T(8,128)} %get-tuple-element.7.b_ref, f32[2,96,256]{2,1,0:T(8,128)} %get-tuple-element.8.a_ref), custom_call_target="tpu_custom_call" | custom-call | tf_op jit(solution)/shard_map/last/pallas_call | solution.py:499

commit v3 on v2

--- a/solution.py
+++ b/solution.py
@@ -13,26 +13,35 @@
 BLK = 256
 NX, NY, NZ = 4, 4, 8
 CH = NX * NZ
-PART = ((0, 160), (160, 224))
+PART = ((0, 160), (160, 112), (272, 112))
+LATER = range(1, len(PART))
+ROWS0, ROWS1 = PART[0][1], max(rows for _, rows in PART[1:])
 LEN = ((4, 3), (4, 3), (3, 4), (3, 4), (4, 3))
 
 ORDER = (
-    ("x0", 1), ("x0", 3), ("z1", 0, 1), ("z1", 1, 1), ("x0", 2), ("apass",), ("x1", 0), ("z0", 0, 0, 1),
-    ("z0", 0, 1, 1), ("z0", 1, 0, 1), ("z0", 1, 1, 1), ("aturn",), ("x1", -1), ("terms", 0), ("z1", 0, 2),
-    ("z1", 1, 2), ("x1", 1), ("z0", 3, 0, 1), ("z0", 2, 1, 1), ("terms", 1), ("z0", 0, 0, 2), ("z0", 0, 1, 2),
-    ("z0", 2, 0, 1), ("terms", 2), ("z0", 1, 0, 2), ("z0", 1, 1, 2), ("z0", 3, 1, 1), ("terms", 3), ("z1", 0, 3),
-    ("z1", 1, 3), ("x1", -2), ("x1", 2), ("z0", 2, 1, 2), ("z0", 0, 0, 3), ("z0", 0, 1, 3), ("z0", 3, 0, 2),
-    ("bpart", 0), ("z0", 1, 1, 3), ("z0", 2, 0, 2), ("z0", 3, 1, 2), ("z0", 1, 0, 3), ("x1", -3), ("z1", 0, 4),
-    ("z0", 2, 1, 3), ("r0", 0, 0, 0), ("r0", 0, 1, 0), ("r0", 1, 0, 0), ("r0", 1, 1, 0), ("u", 4), ("x1", 3),
-    ("r0", 2, 0, 0), ("r0", 2, 1, 0), ("r0", 3, 0, 0), ("r0", 3, 1, 0), ("z0", 0, 0, 4), ("z0", 1, 0, 4),
-    ("z0", 2, 0, 3), ("z0", 3, 0, 3), ("u", -3), ("z0", 2, 1, 4), ("z0", 3, 1, 3), ("bpart", 1), ("r0", 0, 0, 1),
-    ("x1", -4), ("u", 3), ("r0", 0, 1, 1), ("r0", 1, 0, 1), ("r0", 1, 1, 1), ("u", -2), ("r0", 2, 0, 1),
-    ("r0", 2, 1, 1), ("r0", 3, 0, 1), ("r0", 3, 1, 1), ("upass", 4), ("bpart", 2), ("z0", 3, 1, 4), ("r0", 0, 0, 2),
-    ("u", 2), ("bpart", 3), ("orb",), ("r0", 0, 1, 2), ("r0", 1, 0, 2), ("r0", 1, 1, 2), ("r0", 2, 0, 2),
-    ("r0", 2, 1, 2), ("r0", 3, 0, 2), ("r0", 3, 1, 2), ("r0", 0, 0, 3), ("r1", 0, 0), ("upass", -3), ("upass", 3),
-    ("r0", 1, 0, 3), ("upass", -2), ("upass", 2), ("u", -1), ("r0", 2, 1, 3), ("r0", 3, 1, 3), ("u", 1), ("r1", 1, 0),
-    ("orb2",), ("u", 0), ("r1", 0, 1), ("r0x", 1), ("r0x", 2), ("r0x", 3), ("upass", -1), ("upass", 1), ("r1", 1, 1),
-    ("upass", 0), ("r1", 0, 2), ("orb4",), ("r1", 1, 2), ("end0",), ("r1", 0, 3), ("orbend",), ("end1",),
+    ("z1", 1, 1, 1), ("z1", 1, 0, 1), ("z1", 2, 1, 1), ("z1", 2, 0, 1), ("x0", 1), ("x0", 3), ("apass",),
+    ("x1", 1, 0), ("x1", 2, 0), ("x0", 2), ("z1", 1, 1, 2), ("z0", 0, 1, 1), ("x1", 1, 1), ("z1", 1, 0, 2),
+    ("z0", 0, 0, 1), ("x1", 1, -1), ("z1", 2, 0, 2), ("z1", 2, 1, 2), ("aturn",), ("terms", 0), ("z0", 3, 1, 1),
+    ("z0", 1, 0, 1), ("terms", 1), ("z1", 1, 1, 3), ("z0", 2, 0, 1), ("z0", 1, 1, 1), ("z0", 3, 0, 1), ("x1", 2, 1),
+    ("z0", 2, 1, 1), ("z1", 1, 0, 3), ("x1", 1, 2), ("x1", 1, -2), ("terms", 2), ("z1", 2, 1, 3), ("x1", 2, -1),
+    ("z0", 0, 1, 2), ("z1", 2, 0, 3), ("x1", 2, -2), ("z0", 3, 1, 2), ("z0", 1, 0, 2), ("z0", 0, 0, 2), ("terms", 3),
+    ("u", 1, 4), ("r0", 2, 1, 0), ("z0", 2, 1, 2), ("u", 1, 3), ("x1", 2, 2), ("r0", 3, 1, 0), ("u", 2, 4),
+    ("z0", 2, 0, 2), ("r0", 1, 0, 0), ("z0", 3, 0, 2), ("z1", 2, 0, 4), ("u", 2, -3), ("z1", 1, 0, 4), ("x1", 1, -3),
+    ("r0", 2, 0, 0), ("r0", 0, 0, 0), ("r0", 0, 1, 0), ("x1", 2, -3), ("bpart", 0), ("z0", 3, 1, 3), ("x1", 1, 3),
+    ("r0", 3, 0, 0), ("z0", 1, 1, 2), ("z0", 2, 0, 3), ("x1", 2, 3), ("u", 1, 2), ("z0", 0, 0, 3), ("r0", 2, 1, 1),
+    ("r0", 1, 1, 0), ("upass", 1, 4), ("z0", 2, 1, 3), ("r0", 3, 1, 1), ("z0", 1, 0, 3), ("z0", 0, 1, 3), ("u", 2, 2),
+    ("upass", 2, 4), ("bpart", 1), ("r0", 0, 1, 1), ("x1", 2, -4), ("x1", 1, -4), ("u", 2, 3), ("r0", 1, 0, 1),
+    ("u", 1, -3), ("upass", 1, 2), ("upass", 1, 3), ("z0", 3, 1, 4), ("r0", 0, 0, 1), ("upass", 2, -3),
+    ("r0", 2, 0, 1), ("r1", 1, 0, 0), ("u", 2, -2), ("u", 2, -1), ("r0", 3, 0, 1), ("z0", 3, 0, 3), ("z0", 1, 1, 3),
+    ("upass", 2, 2), ("u", 1, -1), ("u", 1, 1), ("r0", 2, 1, 2), ("bpart", 2), ("r0", 1, 1, 1), ("r1", 2, 0, 0),
+    ("z0", 1, 0, 4), ("z0", 2, 1, 4), ("z0", 0, 0, 4), ("upass", 2, 3), ("bpart", 3), ("r0", 3, 1, 2),
+    ("r0", 1, 0, 2), ("orb", 0), ("r0", 0, 1, 2), ("r0", 0, 0, 2), ("r0", 2, 0, 2), ("r0", 2, 1, 3), ("upass", 1, -3),
+    ("r1", 1, 0, 1), ("orb", 1), ("r0", 1, 1, 2), ("r0", 3, 1, 3), ("u", 1, -2), ("r0", 3, 0, 2), ("upass", 1, -1),
+    ("r0", 1, 0, 3), ("r1", 2, 1, 0), ("upass", 2, -2), ("u", 2, 1), ("r1", 2, 0, 1), ("u", 1, 0), ("upass", 2, -1),
+    ("r1", 1, 1, 0), ("u", 2, 0), ("orb2", 0), ("upass", 1, -2), ("r0x", 2), ("orb2", 1), ("r1", 2, 1, 1),
+    ("upass", 1, 1), ("r1", 1, 0, 2), ("r1", 2, 0, 2), ("r0x", 1), ("upass", 1, 0), ("upass", 2, 1), ("r0x", 3),
+    ("r1", 1, 1, 1), ("upass", 2, 0), ("orb4", 0), ("r0", 0, 0, 3), ("r1", 1, 0, 3), ("orb4", 1), ("r1", 2, 1, 2),
+    ("r1", 2, 0, 3), ("r1", 1, 1, 2), ("end0",), ("orbend", 0), ("end1", 2), ("end1", 1), ("orbend", 1),
 )
 
 
@@ -162,14 +171,16 @@
     brow2 = pl.multiple_of(96 * other, 16)
     for h in range(2):
         got(bbuf.at[p, pl.ds(pl.multiple_of(192 * h + 96 * other, 16), 96)], wrecv.at[h])
+    for h in LATER:
+        gsend_to(h, p, zup)
+        gsend_to(h, p, zdown)
     for k in (1, 3, 2):
         gsend_to(0, p, dev(k, 0, 0))
-    gsend_to(1, p, zup)
-    gsend_to(1, p, zdown)
     gsend_to(0, p, zup)
     gsend_to(0, p, zdown)
-    for k in (1, 3):
-        gsend_to(1, p, dev(k, 0, 0))
+    for h in LATER:
+        for k in (1, 3):
+            gsend_to(h, p, dev(k, 0, 0))
     margin_piece(2)
     margin_piece(3)
 
@@ -184,26 +195,27 @@
         if s < LEN[k][way]:
             gsend_to(0, idx, zdown if way else zup)
 
-    def do_z1(way, s):
+    def do_z1(h, way, s):
         idx = chip(0, s if way else -s)
-        gwait(1, idx)
+        gwait(h, idx)
         if s < LEN[4][way]:
-            gsend_to(1, idx, zdown if way else zup)
+            gsend_to(h, idx, zdown if way else zup)
         for k in (1, 3):
-            gsend_to(1, idx, dev(k, 0, 0))
+            gsend_to(h, idx, dev(k, 0, 0))
 
     def offsets(s):
         return (0,) if s == 0 else (-s, s) if s < 4 else (-s,)
 
-    def do_x1(off):
+    def do_x1(h, off):
         odd_chunk = (z + off + NZ) % 2
-        gwait(1, chip(1, off))
-        gwait(1, chip(3, off))
-        gsend_to(1, chip(3 - 2 * odd_chunk, off), dev(1 + 2 * odd_chunk, 0, 0))
+        gwait(h, chip(1, off))
+        gwait(h, chip(3, off))
+        gsend_to(h, chip(3 - 2 * odd_chunk, off), dev(1 + 2 * odd_chunk, 0, 0))
 
     def gather_last(s):
         for off in offsets(s):
-            gwait(1, chip(2, off))
+            for h in LATER:
+                gwait(h, chip(2, off))
 
     ccol = pl.multiple_of(c * BLK, BLK)
 
@@ -270,125 +282,139 @@
         odd_chunk = (z + off + NZ) % 2
         return 1 + 2 * odd_chunk, 3 - 2 * odd_chunk
 
-    def do_u(off):
-        i = 3 * order.index(off)
+    def uref(h, off, j):
+        i = 24 * (h - 1) + 3 * order.index(off) + j
+        return ubuf.at[i, pl.ds(0, PART[h][1])], urecv.at[i]
+
+    def usend(src, h, off, j, k):
+        dst, sem = uref(h, off, j)
+        send(src, dst, rsend, sem, dev(k, 0, 0))
+
+    def do_u(h, off):
         ahead, back = ways(off)
-        send(t_at(1, chip(2, off)), ubuf.at[i], rsend, urecv.at[i], dev(ahead, 0, 0))
-        send(t_at(1, chip(back, off)), ubuf.at[i + 1], rsend, urecv.at[i + 1], dev(back, 0, 0))
-
-    def do_upass(off):
-        i = 3 * order.index(off)
+        usend(t_at(h, chip(2, off)), h, off, 0, ahead)
+        usend(t_at(h, chip(back, off)), h, off, 1, back)
+
+    def do_upass(h, off):
         ahead, _ = ways(off)
-        got(ubuf.at[i], urecv.at[i])
-        ubuf[i] = (ubuf[i].astype(F32) + t_val(1, chip(ahead, off))).astype(BF16)
-        send(ubuf.at[i], ubuf.at[i + 2], rsend, urecv.at[i + 2], dev(ahead, 0, 0))
-
-    def usum(off):
-        total = t_val(1, chip(0, off))
-        i = 3 * order.index(off)
-        for j in (i + 1, i + 2):
-            got(ubuf.at[j], urecv.at[j])
-            total += ubuf[j].astype(F32)
+        ref, sem = uref(h, off, 0)
+        got(ref, sem)
+        ref[...] = (ref[...].astype(F32) + t_val(h, chip(ahead, off))).astype(BF16)
+        usend(ref, h, off, 2, ahead)
+
+    def usum(h, off):
+        total = t_val(h, chip(0, off))
+        for j in (1, 2):
+            ref, sem = uref(h, off, j)
+            got(ref, sem)
+            total += ref[...].astype(F32)
         return total
 
-    def zref(k, way, s):
-        if k == 4:
-            return zbuf1.at[4 * way + s], zrecv.at[32 + 4 * way + s]
+    def zref(h, k, way, s):
+        if h:
+            slot = 8 * (h - 1) + 4 * way + s
+            return zbuf1.at[slot, pl.ds(0, PART[h][1])], zrecv.at[32 + slot]
         slot = 8 * k + 4 * way + s
         return zbuf.at[slot], zrecv.at[slot]
 
-    def zsend(src, k, way, s):
-        dst, sem = zref(k, way, s)
+    def zsend(src, h, k, way, s):
+        dst, sem = zref(h, k, way, s)
         send(src, dst, rsend, sem, zup if way == 0 else zdown)
 
     def do_r0(k, way, s):
         lim = LEN[k][way]
         idx = chip(k, (s - lim) if way else (lim - s))
         if s == 0:
-            zsend(t_at(0, idx), k, way, 0)
+            zsend(t_at(0, idx), 0, k, way, 0)
         else:
-            ref, sem = zref(k, way, s - 1)
+            ref, sem = zref(0, k, way, s - 1)
             got(ref, sem)
             ref[...] = (ref[...].astype(F32) + t_val(0, idx)).astype(BF16)
-            zsend(ref, k, way, s)
-
-    def do_r1(way, s):
+            zsend(ref, 0, k, way, s)
+
+    def do_r1(h, way, s):
         lim = LEN[4][way]
         off = (s - lim) if way else (lim - s)
-        total = usum(off)
+        total = usum(h, off)
         if s > 0:
-            ref, sem = zref(4, way, s - 1)
+            ref, sem = zref(h, 4, way, s - 1)
             got(ref, sem)
             total += ref[...].astype(F32)
-        mine = ubuf.at[3 * order.index(off) + 1]
+        mine = uref(h, off, 1)[0]
         mine[...] = total.astype(BF16)
-        zsend(mine, 4, way, s)
+        zsend(mine, h, 4, way, s)
 
     def plane():
         return [(4 * dx + dy, dx, dy) for dx in range(NX) for dy in range(NY) if dx or dy]
 
-    def do_orb():
-        b_all = bacc[...]
-        high = b_all.astype(BF16)
-        low = (b_all - high.astype(F32)).astype(BF16)
-        bpart[...] = high.reshape(2, NY, 96, BLK)
-        orb = jnp.dot(at[...], high, preferred_element_type=F32)
-        orb += jnp.dot(at[...], low, preferred_element_type=F32)
-        orb = orb.reshape(16, 32, BLK)
-        of32[...] = orb
-        obf[...] = orb.astype(BF16)
+    def strip(a):
+        return pl.ds(16 * a, 16)
+
+    def do_orb(a):
+        if a == 0:
+            b_all = bacc[...]
+            high = b_all.astype(BF16)
+            low = (b_all - high.astype(F32)).astype(BF16)
+            bpart[...] = high.reshape(2, NY, 96, BLK)
+            orb = jnp.dot(at[...], high, preferred_element_type=F32)
+            orb += jnp.dot(at[...], low, preferred_element_type=F32)
+            orb = orb.reshape(16, 32, BLK)
+            of32[...] = orb
+            obf[...] = orb.astype(BF16)
         for slot, dx, dy in plane():
-            src = obf.at[up(x + dx, NX) * 4 + up(y + dy, NY)]
-            send(src, ar1.at[slot], osend1, orecv1.at[slot], dev(dx, 0, dy))
-        for dy in range(NY):
-            for oc in range(2):
-                if dy or oc:
-                    core = c if oc == 0 else other
-                    slot = 2 * dy + oc
-                    src = bpart.at[core, up(y + dy, NY)]
-                    send(src, bslots.at[slot], bsend, brecv.at[slot], dev(0, 0, dy, core))
-        bslots[0] = bpart[c, y]
-
-    def do_orb2():
-        total = of32[4 * x + y]
+            src = obf.at[up(x + dx, NX) * 4 + up(y + dy, NY), strip(a)]
+            send(src, ar1.at[slot, strip(a)], osend1, orecv1.at[16 * a + slot], dev(dx, 0, dy))
+        if a == 1:
+            for dy in range(NY):
+                for oc in range(2):
+                    if dy or oc:
+                        core = c if oc == 0 else other
+                        slot = 2 * dy + oc
+                        src = bpart.at[core, up(y + dy, NY)]
+                        send(src, bslots.at[slot], bsend, brecv.at[slot], dev(0, 0, dy, core))
+            bslots[0] = bpart[c, y]
+
+    def do_orb2(a):
+        total = of32[4 * x + y, strip(a), :]
         for slot, _, _ in plane():
-            got(ar1.at[slot], orecv1.at[slot])
-            total += ar1[slot].astype(F32)
-        az[z] = total.astype(BF16)
+            got(ar1.at[slot, strip(a)], orecv1.at[16 * a + slot])
+            total += ar1[slot, strip(a), :].astype(F32)
+        mine = az.at[z, strip(a)]
+        mine[...] = total.astype(BF16)
         for dz in (4, 3, 5, 2, 6, 1, 7):
-            send(az.at[z], az.at[z], osend2, orecv2.at[dz], dev(0, dz, 0))
-
-    def do_orb4():
+            send(mine, mine, osend2, orecv2.at[8 * a + dz], dev(0, dz, 0))
+
+    def do_orb4(a):
         for dz in range(1, NZ):
-            got(az.at[up(z - dz + NZ, NZ)], orecv2.at[dz])
-        total = az[0].astype(F32)
+            got(az.at[up(z - dz + NZ, NZ), strip(a)], orecv2.at[8 * a + dz])
+        total = az[0, strip(a), :].astype(F32)
         for i in range(1, NZ):
-            total += az[i].astype(F32)
-        mine = rbuf.at[c, 4 * x + y]
+            total += az[i, strip(a), :].astype(F32)
+        mine = rbuf.at[c, 4 * x + y, strip(a)]
         mine[...] = (total * (1.0 / math.sqrt(24576))).astype(BF16)
         for slot, dx, dy in plane():
-            send(mine, mine, osend4, orecv4.at[slot], dev(dx, 0, dy))
-
-    def zlast(k):
-        total = t_val(0, chip(k, 0)) if k < 4 else usum(0)
+            send(mine, mine, osend4, orecv4.at[16 * a + slot], dev(dx, 0, dy))
+
+    def zlast(h, k):
+        total = usum(h, 0) if h else t_val(0, chip(k, 0))
         for way in range(2):
-            ref, sem = zref(k, way, LEN[k][way] - 1)
+            ref, sem = zref(h, k, way, LEN[k][way] - 1)
             got(ref, sem)
             total += ref[...].astype(F32)
         return total
 
     def do_r0x(k):
-        xbuf[k] = zlast(k).astype(BF16)
+        xbuf[k] = zlast(0, k).astype(BF16)
         send(xbuf.at[k], xbuf.at[3 + k], rsend, xrecv.at[k], dev(k, 0, 0))
 
-    halves = []
+    pieces = {}
 
     def do_end0():
-        total = zlast(0)
+        total = zlast(0, 0)
         for k in (1, 3, 2):
             got(xbuf.at[3 + k], xrecv.at[k])
             total += xbuf[3 + k].astype(F32)
-        halves.append(total)
+        pieces[0] = total
         for oc in range(2):
             total = 0.0
             for dy in range(NY):
@@ -399,13 +425,15 @@
             bwhole[c if oc == 0 else other] = total
         pltpu.make_async_copy(bwhole, b_out, outsem.at[0]).start()
 
-    def do_end1():
-        halves.append(zlast(4))
-
-    def do_orbend():
+    def do_end1(h):
+        pieces[h] = zlast(h, 4)
+
+    def do_orbend(a):
         for slot, dx, dy in plane():
-            got(rbuf.at[c, up(x - dx + NX, NX) * 4 + up(y - dy + NY, NY)], orecv4.at[slot])
-        send(rbuf.at[c], rbuf.at[c], dsend, drecv, sib)
+            src = up(x - dx + NX, NX) * 4 + up(y - dy + NY, NY)
+            got(rbuf.at[c, src, strip(a)], orecv4.at[16 * a + slot])
+        half = rbuf.at[c, pl.ds(0, 16), strip(a)]
+        send(half, half, dsend, drecv.at[a], sib)
 
     steps = dict(
         x0=do_x0, z0=do_z0, z1=do_z1, x1=do_x1, apass=do_apass, aturn=do_aturn, terms=do_terms, bpart=do_bpart,
@@ -415,7 +443,7 @@
     for name, *where in ORDER:
         steps[name](*where)
 
-    image = jnp.concatenate(halves, axis=0)
+    image = jnp.concatenate([pieces[h] for h in range(len(PART))], axis=0)
     for h in range(2):
         lanes = pl.ds(128 * h, 128)
         packed = image[192 * h + 128:192 * h + 192, :]
@@ -423,7 +451,8 @@
         aimg[pl.ds(pl.multiple_of(64 * odd, 8), 128), lanes] = image[192 * h:192 * h + 128, :].T
         aimg[pl.ds(pl.multiple_of(128 * (1 - odd), 8), 64), lanes] = rest[0:64, :]
     send(aimg.at[pl.ds(pl.multiple_of(96 * other, 8), 96)], aother, ssend, srecv, sib)
-    got(rbuf.at[other], drecv)
+    for a in range(2):
+        got(rbuf.at[other, pl.ds(0, 16), strip(a)], drecv.at[a])
     pltpu.make_async_copy(rbuf, r_out, outsem.at[1]).start()
     awhole[c] = aimg[pl.ds(brow, 96), :]
     got(aother, srecv)
@@ -466,6 +495,7 @@
 def local(margin, margin_pattern, orbitals_a, pattern_a, orbitals_b, pattern_b):
     vmem, smem, any_ = (pl.BlockSpec(memory_space=s) for s in (pltpu.VMEM, pltpu.SMEM, pl.ANY))
     dma = pltpu.SemaphoreType.DMA
+    later = len(LATER)
 
     def buf(*shape, dtype=BF16):
         return pltpu.VMEM(shape, dtype)
@@ -481,15 +511,15 @@
         out_specs=(any_, any_, any_),
         scratch_shapes=[
             buf(768, 6144), buf(768, 512), buf(512, 768), buf(32, 384, 128), buf(2, 96, 128), buf(32, 384, 128),
-            buf(32, 160, 128), buf(8, 224, 128), buf(24, 224, 128), buf(7, 160, 128),
+            buf(32, ROWS0, 128), buf(8 * later, ROWS1, 128), buf(24 * later, ROWS1, 128), buf(7, ROWS0, 128),
             buf(768, 256, dtype=F32), buf(2, 4, 96, 256), buf(8, 96, 256),
             buf(16, 32, 256, dtype=F32), buf(16, 32, 256), buf(16, 32, 256),
             buf(8, 32, 256), buf(2, 16, 32, 256), buf(192, 256, dtype=F32), buf(96, 256, dtype=F32),
             buf(2, 96, 256, dtype=F32), buf(2, 96, 256, dtype=F32),
             buf(96, 512), buf(96, 512), pltpu.SMEM((96, 96), jnp.int32),
-            dma, dma((3,)), dma, dma((4,)), dma, dma((8,)), dma, dma((2,)), dma, dma((64,)),
-            dma, dma((40,)), dma((24,)), dma((4,)), dma, dma((8,)), dma, dma((16,)), dma, dma((8,)),
-            dma, dma((16,)), dma, dma, dma, dma, dma((3,)),
+            dma, dma((3,)), dma, dma((4,)), dma, dma((8,)), dma, dma((2,)), dma, dma((CH * len(PART),)),
+            dma, dma((32 + 8 * later,)), dma((24 * later,)), dma((4,)), dma, dma((8,)), dma, dma((32,)), dma, dma((16,)),
+            dma, dma((32,)), dma, dma((2,)), dma, dma, dma((3,)),
         ],
         compiler_params=pltpu.CompilerParams(
             collective_id=0, has_side_effects=True, vmem_limit_bytes=60 << 20

time: 67.9 us -> 65.9 us (0.971)
  Pallas kernels: 67.2 us -> 65.1 us
    pallas_call x1, Pallas kernels: 64.4 us -> 62.3 us  [local(): pl.pallas_call(kernel, out_shape=(jax.ShapeDtypeStruct((2, 16, 32, 256),...]
where the time goes in v3:
time: 65.9 us; the launch traced here: 65.8 us
  Pallas kernels  65.1 us (99%)
    pallas_call x1, Pallas kernels, local(): pl.pallas_call(kernel, out_shape=(jax.ShapeDtypeStruct((2, 16, 32, 256),...  62.3 us
    pallas_call x1, Pallas kernels, local(): pl.pallas_call(last_kernel, out_shape=(jax.ShapeDtypeStruct((96, 512), BF...  2.82 us

profile of v3, /device:TPU:1, one launch (start us, length us, event | category | flops | bytes accessed | tf_op | source)
XLA Modules:
  0.0 65.8 jit_solution(12889315995381116277)
XLA Ops:
  0.6 62.3 %exchange.1 = (bf16[2,16,32,256]{3,2,1,0:T(8,128)(2,1)}, f32[2,96,256]{2,1,0:T(8,128)}, f32[2,96,256]{2,1,0:T(8,128)}) custom-call(bf16[384,6144]{1,0:T(8,128)(2,1)} %m_ref.1, s32[96,96]{1,0:T(8,128)} %pm_hbm.1, bf16[96,512]{1,0:T(8,128)(2,1)} %a_hbm.1, s32[2,96]{1,0:T(2,128)} %bitcast.2, bf16[96,512]{1,0:T(8,128)(2,1)} %b_hbm.1, s32[2,96]{1,0:T(2,128)} %bitcast.3), custom_call_target="tpu_custom_call" | custom-call | tf_op jit(solution)/shard_map/exchange/pallas_call | solution.py:503
  62.9 2.8 %last.1 = (bf16[96,512]{1,0:T(8,128)(2,1)}, bf16[96,512]{1,0:T(8,128)(2,1)}, f32[512,512]{1,0:T(8,128)}) custom-call(bf16[2,16,32,256]{3,2,1,0:T(8,128)(2,1)} %get-tuple-element.6.r_ref, f32[2,96,256]{2,1,0:T(8,128)} %get-tuple-element.7.b_ref, f32[2,96,256]{2,1,0:T(8,128)} %get-tuple-element.8.a_ref), custom_call_target="tpu_custom_call" | custom-call | tf_op jit(solution)/shard_map/last/pallas_call | solution.py:529

commit v4 on v3

--- a/solution.py
+++ b/solution.py
@@ -13,40 +13,51 @@
 BLK = 256
 NX, NY, NZ = 4, 4, 8
 CH = NX * NZ
-PART = ((0, 160), (160, 112), (272, 112))
+PART = ((0, 160), (160, 128), (288, 96))
+USED = tuple(start // 2 for start, _ in PART)
 LATER = range(1, len(PART))
 ROWS0, ROWS1 = PART[0][1], max(rows for _, rows in PART[1:])
 LEN = ((4, 3), (4, 3), (3, 4), (3, 4), (4, 3))
 
 ORDER = (
-    ("z1", 1, 1, 1), ("z1", 1, 0, 1), ("z1", 2, 1, 1), ("z1", 2, 0, 1), ("x0", 1), ("x0", 3), ("apass",),
-    ("x1", 1, 0), ("x1", 2, 0), ("x0", 2), ("z1", 1, 1, 2), ("z0", 0, 1, 1), ("x1", 1, 1), ("z1", 1, 0, 2),
-    ("z0", 0, 0, 1), ("x1", 1, -1), ("z1", 2, 0, 2), ("z1", 2, 1, 2), ("aturn",), ("terms", 0), ("z0", 3, 1, 1),
-    ("z0", 1, 0, 1), ("terms", 1), ("z1", 1, 1, 3), ("z0", 2, 0, 1), ("z0", 1, 1, 1), ("z0", 3, 0, 1), ("x1", 2, 1),
-    ("z0", 2, 1, 1), ("z1", 1, 0, 3), ("x1", 1, 2), ("x1", 1, -2), ("terms", 2), ("z1", 2, 1, 3), ("x1", 2, -1),
-    ("z0", 0, 1, 2), ("z1", 2, 0, 3), ("x1", 2, -2), ("z0", 3, 1, 2), ("z0", 1, 0, 2), ("z0", 0, 0, 2), ("terms", 3),
-    ("u", 1, 4), ("r0", 2, 1, 0), ("z0", 2, 1, 2), ("u", 1, 3), ("x1", 2, 2), ("r0", 3, 1, 0), ("u", 2, 4),
-    ("z0", 2, 0, 2), ("r0", 1, 0, 0), ("z0", 3, 0, 2), ("z1", 2, 0, 4), ("u", 2, -3), ("z1", 1, 0, 4), ("x1", 1, -3),
-    ("r0", 2, 0, 0), ("r0", 0, 0, 0), ("r0", 0, 1, 0), ("x1", 2, -3), ("bpart", 0), ("z0", 3, 1, 3), ("x1", 1, 3),
-    ("r0", 3, 0, 0), ("z0", 1, 1, 2), ("z0", 2, 0, 3), ("x1", 2, 3), ("u", 1, 2), ("z0", 0, 0, 3), ("r0", 2, 1, 1),
-    ("r0", 1, 1, 0), ("upass", 1, 4), ("z0", 2, 1, 3), ("r0", 3, 1, 1), ("z0", 1, 0, 3), ("z0", 0, 1, 3), ("u", 2, 2),
-    ("upass", 2, 4), ("bpart", 1), ("r0", 0, 1, 1), ("x1", 2, -4), ("x1", 1, -4), ("u", 2, 3), ("r0", 1, 0, 1),
-    ("u", 1, -3), ("upass", 1, 2), ("upass", 1, 3), ("z0", 3, 1, 4), ("r0", 0, 0, 1), ("upass", 2, -3),
-    ("r0", 2, 0, 1), ("r1", 1, 0, 0), ("u", 2, -2), ("u", 2, -1), ("r0", 3, 0, 1), ("z0", 3, 0, 3), ("z0", 1, 1, 3),
-    ("upass", 2, 2), ("u", 1, -1), ("u", 1, 1), ("r0", 2, 1, 2), ("bpart", 2), ("r0", 1, 1, 1), ("r1", 2, 0, 0),
-    ("z0", 1, 0, 4), ("z0", 2, 1, 4), ("z0", 0, 0, 4), ("upass", 2, 3), ("bpart", 3), ("r0", 3, 1, 2),
-    ("r0", 1, 0, 2), ("orb", 0), ("r0", 0, 1, 2), ("r0", 0, 0, 2), ("r0", 2, 0, 2), ("r0", 2, 1, 3), ("upass", 1, -3),
-    ("r1", 1, 0, 1), ("orb", 1), ("r0", 1, 1, 2), ("r0", 3, 1, 3), ("u", 1, -2), ("r0", 3, 0, 2), ("upass", 1, -1),
-    ("r0", 1, 0, 3), ("r1", 2, 1, 0), ("upass", 2, -2), ("u", 2, 1), ("r1", 2, 0, 1), ("u", 1, 0), ("upass", 2, -1),
-    ("r1", 1, 1, 0), ("u", 2, 0), ("orb2", 0), ("upass", 1, -2), ("r0x", 2), ("orb2", 1), ("r1", 2, 1, 1),
-    ("upass", 1, 1), ("r1", 1, 0, 2), ("r1", 2, 0, 2), ("r0x", 1), ("upass", 1, 0), ("upass", 2, 1), ("r0x", 3),
-    ("r1", 1, 1, 1), ("upass", 2, 0), ("orb4", 0), ("r0", 0, 0, 3), ("r1", 1, 0, 3), ("orb4", 1), ("r1", 2, 1, 2),
-    ("r1", 2, 0, 3), ("r1", 1, 1, 2), ("end0",), ("orbend", 0), ("end1", 2), ("end1", 1), ("orbend", 1),
+    ("z1", 1, 0, 1), ("z1", 1, 1, 1), ("x0", 3), ("z1", 2, 1, 1), ("z1", 2, 0, 1), ("z0", 0, 0, 1), ("z0", 0, 1, 1),
+    ("z1", 1, 0, 2), ("apass",), ("z1", 1, 1, 2), ("x1", 1, 0), ("x0", 1), ("x1", 1, -1), ("x1", 1, 1),
+    ("z1", 2, 0, 2), ("x1", 2, 1), ("z0", 3, 0, 1), ("z0", 3, 1, 1), ("z1", 2, 1, 2), ("x0", 2), ("x1", 2, 0),
+    ("aturn",), ("terms", 0), ("x1", 1, -2), ("z1", 1, 1, 3), ("z0", 0, 0, 2), ("z1", 1, 0, 3), ("terms", 1),
+    ("z1", 2, 0, 3), ("z0", 1, 0, 1), ("x1", 2, -1), ("z0", 1, 1, 1), ("terms", 2), ("z0", 3, 1, 2), ("x1", 1, 2),
+    ("z0", 0, 1, 2), ("z1", 2, 1, 3), ("z0", 2, 0, 1), ("z0", 3, 0, 2), ("terms", 3), ("u", 1, 4), ("z0", 2, 1, 1),
+    ("r0", 2, 1, 0), ("u", 2, 4), ("r0", 0, 0, 0), ("r0", 3, 1, 0), ("r0", 1, 0, 0), ("x1", 2, 2), ("z1", 2, 0, 4),
+    ("x1", 1, 3), ("u", 2, -3), ("z1", 1, 0, 4), ("x1", 2, -2), ("z0", 3, 1, 3), ("x1", 2, -3), ("z0", 1, 0, 2),
+    ("x1", 1, -3), ("z0", 2, 1, 2), ("z0", 0, 0, 3), ("r0", 3, 0, 0), ("upass", 2, 4), ("upass", 1, 4),
+    ("r0", 2, 1, 1), ("x1", 2, 3), ("u", 1, -3), ("x1", 2, -4), ("u", 1, 3), ("z0", 1, 1, 2), ("z0", 2, 0, 2),
+    ("bpart", 0), ("u", 2, 3), ("r0", 1, 1, 0), ("z0", 1, 0, 3), ("r0", 2, 0, 0), ("x1", 1, -4), ("u", 1, -2),
+    ("z0", 3, 1, 4), ("z0", 0, 1, 3), ("z0", 0, 0, 4), ("r0", 1, 0, 1), ("u", 2, -1), ("z0", 3, 0, 3),
+    ("z0", 2, 1, 3), ("r0", 3, 1, 1), ("r0", 0, 0, 1), ("upass", 2, -3), ("bpart", 1), ("r0", 3, 0, 1),
+    ("upass", 1, -3), ("r0", 0, 1, 0), ("z0", 2, 0, 3), ("u", 1, 2), ("u", 2, -2), ("u", 1, -1), ("r0", 2, 1, 2),
+    ("r1", 2, 0, 0), ("upass", 1, 3), ("z0", 1, 1, 3), ("u", 2, 2), ("z0", 1, 0, 4), ("r0", 1, 1, 1), ("r1", 1, 0, 0),
+    ("upass", 2, 3), ("bpart", 2), ("z0", 2, 1, 4), ("r0", 2, 0, 1), ("bpart", 3), ("r0", 1, 0, 2), ("r0", 3, 1, 2),
+    ("upass", 1, -2), ("orb", 0), ("orb", 1), ("r0", 3, 0, 2), ("r0", 2, 1, 3), ("u", 2, 1), ("r0", 1, 1, 2),
+    ("r0", 0, 0, 2), ("r1", 1, 0, 1), ("r1", 2, 1, 0), ("u", 2, 0), ("upass", 2, -2), ("upass", 1, 2),
+    ("upass", 2, 2), ("u", 1, 0), ("u", 1, 1), ("r1", 1, 1, 0), ("r0", 2, 0, 2), ("r0", 0, 1, 1), ("r0", 1, 0, 3),
+    ("r0", 3, 1, 3), ("r1", 2, 0, 1), ("orb2", 0), ("upass", 1, -1), ("orb2", 1), ("r0x", 2), ("r1", 2, 1, 1),
+    ("r0x", 1), ("upass", 2, 1), ("upass", 2, -1), ("upass", 2, 0), ("upass", 1, 1), ("r1", 2, 0, 2), ("r1", 1, 1, 1),
+    ("r1", 1, 0, 2), ("r0", 0, 0, 3), ("upass", 1, 0), ("r0", 0, 1, 2), ("r0x", 3), ("orb4", 0), ("r1", 2, 1, 2),
+    ("orb4", 1), ("r1", 2, 0, 3), ("r1", 1, 0, 3), ("r1", 1, 1, 2), ("end0",), ("orbend", 0), ("end1", 2),
+    ("end1", 1), ("orbend", 1),
 )
 
 
 def up(v, n):
     return lax.rem(v, n)
+
+
+def spots(core, block):
+    found = []
+    for (start, rows), used in zip(PART, USED):
+        low, high = max(used, 96 * block), min(used + rows // 2, 96 * block + 96)
+        if low < high:
+            found.append((start + core * rows // 2 + low - used, high - low))
+    return found
 
 
 def contract0(a, b):
@@ -62,7 +73,7 @@
     m_ref, pm_hbm, a_hbm, pa_ref, b_hbm, pb_ref,
     r_out, b_out, a_out,
     mbuf, afull, at, bbuf, bst, terms, zbuf, zbuf1, ubuf, xbuf, bacc, bpart, bslots,
-    of32, obf, ar1, az, rbuf, aimg, aother, bwhole, awhole, a_ref, b_ref, pm_ref,
+    of32, obf, ar1, az, rbuf, aimg, aother, bwhole, a_ref, b_ref, pm_ref,
     lsem, insem, msend, mrecv, asend, arecv, wsend, wrecv, gsend, grecv,
     rsend, zrecv, urecv, xrecv, bsend, brecv, osend1, orecv1, osend2, orecv2,
     osend4, orecv4, dsend, drecv, ssend, srecv, outsem,
@@ -91,7 +102,9 @@
     sib = dev(0, 0, 0, other)
     zup, zdown = dev(0, 1, 0), dev(0, -1, 0)
 
-    partners = [sib, zup, zdown] + [dev(k, 0, 0) for k in (1, 2, 3)] + [dev(0, 0, k) for k in (1, 2, 3)]
+    partners = [sib] + [dev(0, 0, k) for k in (1, 2, 3)]
+    for core in (c, other):
+        partners += [dev(0, 1, 0, core), dev(0, -1, 0, core)] + [dev(k, 0, 0, core) for k in (1, 2, 3)]
     bar = pltpu.get_barrier_semaphore()
     for to in partners:
         pl.semaphore_signal(bar, inc=1, device_id=to, device_id_type=MESH)
@@ -118,10 +131,18 @@
     here = jnp.where(c == 0, b0.astype(F32), b1.astype(F32)).astype(BF16)
     there = jnp.where(c == 0, b1.astype(F32), b0.astype(F32)).astype(BF16)
     brow = pl.multiple_of(96 * c, 16)
-    for h in range(2):
-        bbuf[p, pl.ds(pl.multiple_of(192 * h + 96 * c, 16), 96), :] = here[:, h * 128:(h + 1) * 128]
-        bst[h, :, :] = there[:, h * 128:(h + 1) * 128]
-
+    here = jnp.concatenate([here[:, 0:128], here[:, 128:256]], axis=0)
+    bst[...] = jnp.concatenate([there[:, 0:128], there[:, 128:256]], axis=0)
+
+    def own_piece(h):
+        start, rows = PART[h]
+        return bbuf.at[p, pl.ds(pl.multiple_of(start + c * (rows // 2), 16), rows // 2)]
+
+    def other_piece(h):
+        return bst.at[pl.ds(USED[h], PART[h][1] // 2)]
+
+    for h in range(len(PART)):
+        own_piece(h)[...] = here[USED[h]:USED[h] + PART[h][1] // 2, :]
     loads[1].wait()
     arow = pl.multiple_of(384 * c + 96 * y, 16)
     a0, a1 = masked(a_ref, pa_ref, 4 * r + y)
@@ -129,9 +150,32 @@
     afull[pl.ds(arow, 96), 256:512] = a1
     pl.semaphore_wait(bar, len(partners))
 
-    for h in range(2):
-        piece = bbuf.at[p, pl.ds(pl.multiple_of(192 * h + 96 * c, 16), 96)]
-        send(bst.at[h], piece, wsend, wrecv.at[h], sib)
+    def chunk(h, idx):
+        return bbuf.at[idx, pl.ds(*PART[h])]
+
+    def gsend_to(h, idx, to):
+        send(chunk(h, idx), chunk(h, idx), gsend, grecv.at[h * CH + idx], to)
+
+    def gwait(h, idx):
+        got(chunk(h, idx), grecv.at[h * CH + idx])
+
+    def first_send(h, dx, dz):
+        send(own_piece(h), own_piece(h), gsend, grecv.at[h * CH + p], dev(dx, dz, 0))
+        send(other_piece(h), own_piece(h), gsend, grecv.at[h * CH + p], dev(dx, dz, 0, other))
+
+    for h in LATER:
+        first_send(h, 0, 1)
+        first_send(h, 0, -1)
+    for k in (1, 3, 2):
+        first_send(0, k, 0)
+    first_send(0, 0, 1)
+    first_send(0, 0, -1)
+    for h in LATER:
+        for k in (1, 3):
+            first_send(h, k, 0)
+    for h in range(len(PART)):
+        send(other_piece(h), own_piece(h), wsend, wrecv, sib)
+
     def a_rows(core, dy):
         return afull.at[pl.ds(pl.multiple_of(384 * core + 96 * up(y + NY - dy, NY), 16), 96)]
 
@@ -159,28 +203,6 @@
     margin_piece(0)
     margin_piece(1)
 
-    def chunk(h, idx):
-        return bbuf.at[idx, pl.ds(*PART[h])]
-
-    def gsend_to(h, idx, to):
-        send(chunk(h, idx), chunk(h, idx), gsend, grecv.at[h * CH + idx], to)
-
-    def gwait(h, idx):
-        got(chunk(h, idx), grecv.at[h * CH + idx])
-
-    brow2 = pl.multiple_of(96 * other, 16)
-    for h in range(2):
-        got(bbuf.at[p, pl.ds(pl.multiple_of(192 * h + 96 * other, 16), 96)], wrecv.at[h])
-    for h in LATER:
-        gsend_to(h, p, zup)
-        gsend_to(h, p, zdown)
-    for k in (1, 3, 2):
-        gsend_to(0, p, dev(k, 0, 0))
-    gsend_to(0, p, zup)
-    gsend_to(0, p, zdown)
-    for h in LATER:
-        for k in (1, 3):
-            gsend_to(h, p, dev(k, 0, 0))
     margin_piece(2)
     margin_piece(3)
 
@@ -245,6 +267,7 @@
 
     def do_bpart(i):
         if i == 0:
+            got(bst, wrecv)
             gather_last(0)
         gather_last(i + 1)
         shift = (0, 3 + 2 * odd, 1 + 2 * odd, 2)[i]
@@ -253,7 +276,10 @@
         for k in range(NX):
             first = up(x + k, NX) * NZ + 2 * pair
             tiles.append(mbuf[:, pl.ds(pl.multiple_of(192 * first, 128), 384)])
-            halves = [bbuf[pl.ds(first, 2), 192 * h:192 * h + 192, :].reshape(384, 128) for h in range(2)]
+            halves = []
+            for block in range(2):
+                found = [(e, spot) for e in range(2) for core in range(2) for spot in spots(core, block)]
+                halves.append(jnp.concatenate([bbuf[first + e, a:a + n, :] for e, (a, n) in found], axis=0))
             rows.append(jnp.concatenate(halves, axis=1))
         part = jnp.dot(
             jnp.concatenate(tiles, axis=1), jnp.concatenate(rows, axis=0), preferred_element_type=F32
@@ -451,15 +477,15 @@
         aimg[pl.ds(pl.multiple_of(64 * odd, 8), 128), lanes] = image[192 * h:192 * h + 128, :].T
         aimg[pl.ds(pl.multiple_of(128 * (1 - odd), 8), 64), lanes] = rest[0:64, :]
     send(aimg.at[pl.ds(pl.multiple_of(96 * other, 8), 96)], aother, ssend, srecv, sib)
+    mine = aimg.at[pl.ds(brow, 96)]
+    pltpu.make_async_copy(mine, a_out.at[c], outsem.at[2]).start()
     for a in range(2):
         got(rbuf.at[other, pl.ds(0, 16), strip(a)], drecv.at[a])
     pltpu.make_async_copy(rbuf, r_out, outsem.at[1]).start()
-    awhole[c] = aimg[pl.ds(brow, 96), :]
     got(aother, srecv)
-    awhole[other] = aother[...]
-    pltpu.make_async_copy(awhole, a_out, outsem.at[2]).start()
-
-    for i, (src, dst) in enumerate(((bwhole, b_out), (rbuf, r_out), (awhole, a_out))):
+    pltpu.make_async_copy(aother, a_out.at[other], outsem.at[3]).start()
+
+    for i, (src, dst) in enumerate(((bwhole, b_out), (rbuf, r_out), (mine, a_out.at[c]), (aother, a_out.at[other]))):
         pltpu.make_async_copy(src, dst, outsem.at[i]).wait()
     got(bst, wsend)
     got(afull.at[pl.ds(0, 672)], asend)
@@ -474,26 +500,52 @@
     got(aother, ssend)
 
 
-def last_kernel(r_ref, b_ref, a_ref, oa_ref, ob_ref, oo_ref):
+def last_kernel(
+    r_hbm, b_hbm, a_hbm, oa_hbm, ob_hbm, oo_hbm, r_ref, b_ref, a_ref, oa_ref, ob_ref, oo_ref, insem, outsem
+):
     factor = 1.0 / math.sqrt(512)
-    res_a, res_b = 0.0, [0.0, 0.0]
-    for h in range(2):
-        oo_ref[:, h * BLK:(h + 1) * BLK] = r_ref[h].reshape(512, BLK).astype(F32)
+    loads = [
+        pltpu.make_async_copy(src, dst, insem.at[i])
+        for i, (src, dst) in enumerate(((r_hbm, r_ref), (b_hbm, b_ref), (a_hbm, a_ref)))
+    ]
+    for load in loads:
+        load.start()
+    stores = []
+
+    def store(src, dst):
+        stores.append(pltpu.make_async_copy(src, dst, outsem.at[len(stores)]))
+        stores[-1].start()
+
+    loads[0].wait()
+    for g in range(2):
+        rows = pl.ds(BLK * g, BLK)
+        for h in range(2):
+            oo_ref[rows, h * BLK:(h + 1) * BLK] = r_ref[h, 8 * g:8 * g + 8].reshape(BLK, BLK).astype(F32)
+        store(oo_ref.at[rows], oo_hbm.at[rows])
+    loads[1].wait()
+    res_a = 0.0
     for h in range(2):
         half = r_ref[h].reshape(512, BLK)
         for v in split(b_ref[h]):
             res_a += lax.dot_general(v, half, (((1,), (1,)), ((), ())), preferred_element_type=F32)
+    oa_ref[...] = (res_a * factor).astype(BF16)
+    store(oa_ref, oa_hbm)
+    loads[2].wait()
+    res_b = [0.0, 0.0]
+    for h in range(2):
         for v in split(a_ref[h]):
             for j in range(2):
                 rows = r_ref[j, 8 * h:8 * h + 8].reshape(BLK, BLK)
                 res_b[j] += jnp.dot(v, rows, preferred_element_type=F32)
-    oa_ref[...] = (res_a * factor).astype(BF16)
     for j in range(2):
         ob_ref[:, j * BLK:(j + 1) * BLK] = (res_b[j] * factor).astype(BF16)
+    store(ob_ref, ob_hbm)
+    for copy in stores:
+        copy.wait()
 
 
 def local(margin, margin_pattern, orbitals_a, pattern_a, orbitals_b, pattern_b):
-    vmem, smem, any_ = (pl.BlockSpec(memory_space=s) for s in (pltpu.VMEM, pltpu.SMEM, pl.ANY))
+    smem, any_ = (pl.BlockSpec(memory_space=s) for s in (pltpu.SMEM, pl.ANY))
     dma = pltpu.SemaphoreType.DMA
     later = len(LATER)
 
@@ -510,16 +562,15 @@
         in_specs=[any_, any_, any_, smem, any_, smem],
         out_specs=(any_, any_, any_),
         scratch_shapes=[
-            buf(768, 6144), buf(768, 512), buf(512, 768), buf(32, 384, 128), buf(2, 96, 128), buf(32, 384, 128),
+            buf(768, 6144), buf(768, 512), buf(512, 768), buf(32, 384, 128), buf(192, 128), buf(32, 384, 128),
             buf(32, ROWS0, 128), buf(8 * later, ROWS1, 128), buf(24 * later, ROWS1, 128), buf(7, ROWS0, 128),
             buf(768, 256, dtype=F32), buf(2, 4, 96, 256), buf(8, 96, 256),
             buf(16, 32, 256, dtype=F32), buf(16, 32, 256), buf(16, 32, 256),
             buf(8, 32, 256), buf(2, 16, 32, 256), buf(192, 256, dtype=F32), buf(96, 256, dtype=F32),
-            buf(2, 96, 256, dtype=F32), buf(2, 96, 256, dtype=F32),
-            buf(96, 512), buf(96, 512), pltpu.SMEM((96, 96), jnp.int32),
-            dma, dma((3,)), dma, dma((4,)), dma, dma((8,)), dma, dma((2,)), dma, dma((CH * len(PART),)),
+            buf(2, 96, 256, dtype=F32), buf(96, 512), buf(96, 512), pltpu.SMEM((96, 96), jnp.int32),
+            dma, dma((3,)), dma, dma((4,)), dma, dma((8,)), dma, dma, dma, dma((CH * len(PART),)),
             dma, dma((32 + 8 * later,)), dma((24 * later,)), dma((4,)), dma, dma((8,)), dma, dma((32,)), dma, dma((16,)),
-            dma, dma((32,)), dma, dma((2,)), dma, dma, dma((3,)),
+            dma, dma((32,)), dma, dma((2,)), dma, dma, dma((4,)),
         ],
         compiler_params=pltpu.CompilerParams(
             collective_id=0, has_side_effects=True, vmem_limit_bytes=60 << 20
@@ -533,8 +584,12 @@
             jax.ShapeDtypeStruct((96, 512), BF16),
             jax.ShapeDtypeStruct((512, 512), F32),
         ),
-        in_specs=[vmem, vmem, vmem],
-        out_specs=(vmem, vmem, vmem),
+        in_specs=[any_, any_, any_],
+        out_specs=(any_, any_, any_),
+        scratch_shapes=[
+            buf(2, 16, 32, 256), buf(2, 96, 256, dtype=F32), buf(2, 96, 256, dtype=F32),
+            buf(96, 512), buf(96, 512), buf(512, 512, dtype=F32), dma((3,)), dma((4,)),
+        ],
         compiler_params=pltpu.CompilerParams(vmem_limit_bytes=60 << 20),
         name="last",
     )(*middle)

time: 65.9 us -> 64.8 us (0.983)
  Pallas kernels: 65.1 us -> 64.1 us
    pallas_call x1, Pallas kernels: 62.3 us -> 61.5 us  [local(): pl.pallas_call(kernel, out_shape=(jax.ShapeDtypeStruct((2, 16, 32, 256),...]
where the time goes in v4:
time: 64.8 us; the launch traced here: 64.7 us
  Pallas kernels  64.1 us (99%)
    pallas_call x1, Pallas kernels, local(): pl.pallas_call(kernel, out_shape=(jax.ShapeDtypeStruct((2, 16, 32, 256),...  61.5 us
    pallas_call x1, Pallas kernels, local(): pl.pallas_call(last_kernel, out_shape=(jax.ShapeDtypeStruct((96, 512), BF...  2.59 us

profile of v4, /device:TPU:1, one launch (start us, length us, event | category | flops | bytes accessed | tf_op | source)
XLA Modules:
  0.0 64.7 jit_solution(10378543942994386090)
XLA Ops:
  0.6 61.5 %exchange.1 = (bf16[2,16,32,256]{3,2,1,0:T(8,128)(2,1)}, f32[2,96,256]{2,1,0:T(8,128)}, f32[2,96,256]{2,1,0:T(8,128)}) custom-call(bf16[384,6144]{1,0:T(8,128)(2,1)} %m_ref.1, s32[96,96]{1,0:T(8,128)} %pm_hbm.1, bf16[96,512]{1,0:T(8,128)(2,1)} %a_hbm.1, s32[2,96]{1,0:T(2,128)} %bitcast.2, bf16[96,512]{1,0:T(8,128)(2,1)} %b_hbm.1, s32[2,96]{1,0:T(2,128)} %bitcast.3), custom_call_target="tpu_custom_call" | custom-call | tf_op jit(solution)/shard_map/exchange/pallas_call | solution.py:555
  62.1 2.6 %last.1 = (bf16[96,512]{1,0:T(8,128)(2,1)}, bf16[96,512]{1,0:T(8,128)(2,1)}, f32[512,512]{1,0:T(8,128)}) custom-call(bf16[2,16,32,256]{3,2,1,0:T(8,128)(2,1)} %get-tuple-element.6.r_hbm, f32[2,96,256]{2,1,0:T(8,128)} %get-tuple-element.7.b_hbm, f32[2,96,256]{2,1,0:T(8,128)} %get-tuple-element.8.a_hbm), custom_call_target="tpu_custom_call" | custom-call | tf_op jit(solution)/shard_map/last/pallas_call | solution.py:580

commit v5 on v4

--- a/solution.py
+++ b/solution.py
@@ -70,10 +70,10 @@
 
 
 def kernel(
-    m_ref, pm_hbm, a_hbm, pa_ref, b_hbm, pb_ref,
+    m_ref, pm_hbm, a_hbm, pa_hbm, b_hbm, pb_hbm,
     r_out, b_out, a_out,
     mbuf, afull, at, bbuf, bst, terms, zbuf, zbuf1, ubuf, xbuf, bacc, bpart, bslots,
-    of32, obf, ar1, az, rbuf, aimg, aother, bwhole, a_ref, b_ref, pm_ref,
+    of32, obf, ar1, az, rbuf, aimg, bwhole, a_ref, b_ref, pm_ref, pa_ref, pb_ref,
     lsem, insem, msend, mrecv, asend, arecv, wsend, wrecv, gsend, grecv,
     rsend, zrecv, urecv, xrecv, bsend, brecv, osend1, orecv1, osend2, orecv2,
     osend4, orecv4, dsend, drecv, ssend, srecv, outsem,
@@ -109,7 +109,8 @@
     for to in partners:
         pl.semaphore_signal(bar, inc=1, device_id=to, device_id_type=MESH)
     loads = []
-    for i, (src, dst) in enumerate(((b_hbm, b_ref), (a_hbm, a_ref), (pm_hbm, pm_ref))):
+    staged = ((b_hbm, b_ref), (a_hbm, a_ref), (pm_hbm, pm_ref), (pb_hbm, pb_ref), (pa_hbm, pa_ref))
+    for i, (src, dst) in enumerate(staged):
         loads.append(pltpu.make_async_copy(src, dst, insem.at[i]))
         loads[-1].start()
     own_m = mbuf.at[pl.ds(pl.multiple_of(c * 384, 128), 384)]
@@ -127,6 +128,7 @@
         return parts
 
     loads[0].wait()
+    loads[3].wait()
     b0, b1 = masked(b_ref, pb_ref, 64 * y + r)
     here = jnp.where(c == 0, b0.astype(F32), b1.astype(F32)).astype(BF16)
     there = jnp.where(c == 0, b1.astype(F32), b0.astype(F32)).astype(BF16)
@@ -144,6 +146,7 @@
     for h in range(len(PART)):
         own_piece(h)[...] = here[USED[h]:USED[h] + PART[h][1] // 2, :]
     loads[1].wait()
+    loads[4].wait()
     arow = pl.multiple_of(384 * c + 96 * y, 16)
     a0, a1 = masked(a_ref, pa_ref, 4 * r + y)
     afull[pl.ds(arow, 96), 0:256] = a0
@@ -449,7 +452,7 @@
                     got(bslots.at[slot], brecv.at[slot])
                 total += bslots[slot].astype(F32)
             bwhole[c if oc == 0 else other] = total
-        pltpu.make_async_copy(bwhole, b_out, outsem.at[0]).start()
+        pltpu.make_async_copy(bwhole, b_out, outsem.at[3]).start()
 
     def do_end1(h):
         pieces[h] = zlast(h, 4)
@@ -458,8 +461,9 @@
         for slot, dx, dy in plane():
             src = up(x - dx + NX, NX) * 4 + up(y - dy + NY, NY)
             got(rbuf.at[c, src, strip(a)], orecv4.at[16 * a + slot])
-        half = rbuf.at[c, pl.ds(0, 16), strip(a)]
-        send(half, half, dsend, drecv.at[a], sib)
+        half, there = rbuf.at[c, pl.ds(0, 16), strip(a)], r_out.at[c, pl.ds(0, 16), strip(a)]
+        send(half, there, dsend, drecv.at[a], sib)
+        pltpu.make_async_copy(half, there, outsem.at[a]).start()
 
     steps = dict(
         x0=do_x0, z0=do_z0, z1=do_z1, x1=do_x1, apass=do_apass, aturn=do_aturn, terms=do_terms, bpart=do_bpart,
@@ -476,17 +480,15 @@
         rest = jnp.concatenate([packed, pltpu.roll(packed, 64, 1)], axis=0).T
         aimg[pl.ds(pl.multiple_of(64 * odd, 8), 128), lanes] = image[192 * h:192 * h + 128, :].T
         aimg[pl.ds(pl.multiple_of(128 * (1 - odd), 8), 64), lanes] = rest[0:64, :]
-    send(aimg.at[pl.ds(pl.multiple_of(96 * other, 8), 96)], aother, ssend, srecv, sib)
+    send(aimg.at[pl.ds(pl.multiple_of(96 * other, 8), 96)], a_out.at[c], ssend, srecv, sib)
     mine = aimg.at[pl.ds(brow, 96)]
     pltpu.make_async_copy(mine, a_out.at[c], outsem.at[2]).start()
     for a in range(2):
-        got(rbuf.at[other, pl.ds(0, 16), strip(a)], drecv.at[a])
-    pltpu.make_async_copy(rbuf, r_out, outsem.at[1]).start()
-    got(aother, srecv)
-    pltpu.make_async_copy(aother, a_out.at[other], outsem.at[3]).start()
-
-    for i, (src, dst) in enumerate(((bwhole, b_out), (rbuf, r_out), (mine, a_out.at[c]), (aother, a_out.at[other]))):
-        pltpu.make_async_copy(src, dst, outsem.at[i]).wait()
+        got(r_out.at[other, pl.ds(0, 16), strip(a)], drecv.at[a])
+        got(r_out.at[c, pl.ds(0, 16), strip(a)], outsem.at[a])
+    got(bwhole, outsem.at[3])
+    got(mine, outsem.at[2])
+
     got(bst, wsend)
     got(afull.at[pl.ds(0, 672)], asend)
     got(own_m, msend)
@@ -497,7 +499,8 @@
     got(obf.at[pl.ds(0, 7)], osend2)
     got(obf.at[pl.ds(0, 15)], osend4)
     got(rbuf.at[c], dsend)
-    got(aother, ssend)
+    got(mine, ssend)
+    got(a_out.at[other], srecv)
 
 
 def last_kernel(
@@ -545,7 +548,7 @@
 
 
 def local(margin, margin_pattern, orbitals_a, pattern_a, orbitals_b, pattern_b):
-    smem, any_ = (pl.BlockSpec(memory_space=s) for s in (pltpu.SMEM, pl.ANY))
+    any_ = pl.BlockSpec(memory_space=pl.ANY)
     dma = pltpu.SemaphoreType.DMA
     later = len(LATER)
 
@@ -559,16 +562,17 @@
             jax.ShapeDtypeStruct((2, 96, 256), F32),
             jax.ShapeDtypeStruct((2, 96, 256), F32),
         ),
-        in_specs=[any_, any_, any_, smem, any_, smem],
+        in_specs=[any_] * 6,
         out_specs=(any_, any_, any_),
         scratch_shapes=[
             buf(768, 6144), buf(768, 512), buf(512, 768), buf(32, 384, 128), buf(192, 128), buf(32, 384, 128),
             buf(32, ROWS0, 128), buf(8 * later, ROWS1, 128), buf(24 * later, ROWS1, 128), buf(7, ROWS0, 128),
             buf(768, 256, dtype=F32), buf(2, 4, 96, 256), buf(8, 96, 256),
             buf(16, 32, 256, dtype=F32), buf(16, 32, 256), buf(16, 32, 256),
-            buf(8, 32, 256), buf(2, 16, 32, 256), buf(192, 256, dtype=F32), buf(96, 256, dtype=F32),
+            buf(8, 32, 256), buf(2, 16, 32, 256), buf(192, 256, dtype=F32),
             buf(2, 96, 256, dtype=F32), buf(96, 512), buf(96, 512), pltpu.SMEM((96, 96), jnp.int32),
-            dma, dma((3,)), dma, dma((4,)), dma, dma((8,)), dma, dma, dma, dma((CH * len(PART),)),
+            pltpu.SMEM((2, 96), jnp.int32), pltpu.SMEM((2, 96), jnp.int32),
+            dma, dma((5,)), dma, dma((4,)), dma, dma((8,)), dma, dma, dma, dma((CH * len(PART),)),
             dma, dma((32 + 8 * later,)), dma((24 * later,)), dma((4,)), dma, dma((8,)), dma, dma((32,)), dma, dma((16,)),
             dma, dma((32,)), dma, dma((2,)), dma, dma, dma((4,)),
         ],

time: 64.8 us -> 63.5 us (0.980)
  Pallas kernels: 64.1 us -> 62.8 us
    pallas_call x1, Pallas kernels: 61.5 us -> 60.2 us  [local(): pl.pallas_call(kernel, out_shape=(jax.ShapeDtypeStruct((2, 16, 32, 256),...]
where the time goes in v5:
time: 63.5 us; the launch traced here: 63.4 us
  Pallas kernels  62.8 us (99%)
  between operations  0.64 us (1%)
    pallas_call x1, Pallas kernels, local(): pl.pallas_call(kernel, out_shape=(jax.ShapeDtypeStruct((2, 16, 32, 256),...  60.2 us
    pallas_call x1, Pallas kernels, local(): pl.pallas_call(last_kernel, out_shape=(jax.ShapeDtypeStruct((96, 512), BF...  2.59 us

profile of v5, /device:TPU:1, one launch (start us, length us, event | category | flops | bytes accessed | tf_op | source)
XLA Modules:
  0.0 63.4 jit_solution(3825385021536986525)
XLA Ops:
  0.6 60.2 %exchange.1 = (bf16[2,16,32,256]{3,2,1,0:T(8,128)(2,1)}, f32[2,96,256]{2,1,0:T(8,128)}, f32[2,96,256]{2,1,0:T(8,128)}) custom-call(bf16[384,6144]{1,0:T(8,128)(2,1)} %m_ref.1, s32[96,96]{1,0:T(8,128)} %pm_hbm.1, bf16[96,512]{1,0:T(8,128)(2,1)} %a_hbm.1, s32[2,96]{1,0:T(2,128)} %bitcast.2, bf16[96,512]{1,0:T(8,128)(2,1)} %b_hbm.1, s32[2,96]{1,0:T(2,128)} %bitcast.3), custom_call_target="tpu_custom_call" | custom-call | tf_op jit(solution)/shard_map/exchange/pallas_call | solution.py:558
  60.8 2.6 %last.1 = (bf16[96,512]{1,0:T(8,128)(2,1)}, bf16[96,512]{1,0:T(8,128)(2,1)}, f32[512,512]{1,0:T(8,128)}) custom-call(bf16[2,16,32,256]{3,2,1,0:T(8,128)(2,1)} %get-tuple-element.6.r_hbm, f32[2,96,256]{2,1,0:T(8,128)} %get-tuple-element.7.b_hbm, f32[2,96,256]{2,1,0:T(8,128)} %get-tuple-element.8.a_hbm), custom_call_target="tpu_custom_call" | custom-call | tf_op jit(solution)/shard_map/last/pallas_call | solution.py:584

commit v6 on v5

--- a/solution.py
+++ b/solution.py
@@ -384,7 +384,6 @@
             b_all = bacc[...]
             high = b_all.astype(BF16)
             low = (b_all - high.astype(F32)).astype(BF16)
-            bpart[...] = high.reshape(2, NY, 96, BLK)
             orb = jnp.dot(at[...], high, preferred_element_type=F32)
             orb += jnp.dot(at[...], low, preferred_element_type=F32)
             orb = orb.reshape(16, 32, BLK)
@@ -393,6 +392,8 @@
         for slot, dx, dy in plane():
             src = obf.at[up(x + dx, NX) * 4 + up(y + dy, NY), strip(a)]
             send(src, ar1.at[slot, strip(a)], osend1, orecv1.at[16 * a + slot], dev(dx, 0, dy))
+        if a == 0:
+            bpart[...] = high.reshape(2, NY, 96, BLK)
         if a == 1:
             for dy in range(NY):
                 for oc in range(2):
@@ -444,6 +445,7 @@
             got(xbuf.at[3 + k], xrecv.at[k])
             total += xbuf[3 + k].astype(F32)
         pieces[0] = total
+        aimg[pl.ds(pl.multiple_of(64 * odd, 8), 128), 0:128] = total[0:128, :].T
         for oc in range(2):
             total = 0.0
             for dy in range(NY):
@@ -478,7 +480,8 @@
         lanes = pl.ds(128 * h, 128)
         packed = image[192 * h + 128:192 * h + 192, :]
         rest = jnp.concatenate([packed, pltpu.roll(packed, 64, 1)], axis=0).T
-        aimg[pl.ds(pl.multiple_of(64 * odd, 8), 128), lanes] = image[192 * h:192 * h + 128, :].T
+        if h:
+            aimg[pl.ds(pl.multiple_of(64 * odd, 8), 128), lanes] = image[192 * h:192 * h + 128, :].T
         aimg[pl.ds(pl.multiple_of(128 * (1 - odd), 8), 64), lanes] = rest[0:64, :]
     send(aimg.at[pl.ds(pl.multiple_of(96 * other, 8), 96)], a_out.at[c], ssend, srecv, sib)
     mine = aimg.at[pl.ds(brow, 96)]

time: 63.5 us -> 63.4 us (level)
  no operation moved by 1% of the time
where the time goes in v6:
time: 63.4 us; the launch traced here: 63.3 us
  Pallas kernels  62.7 us (99%)
  between operations  0.64 us (1%)
    pallas_call x1, Pallas kernels, local(): pl.pallas_call(kernel, out_shape=(jax.ShapeDtypeStruct((2, 16, 32, 256),...  60.1 us
    pallas_call x1, Pallas kernels, local(): pl.pallas_call(last_kernel, out_shape=(jax.ShapeDtypeStruct((96, 512), BF...  2.59 us

profile of v6, /device:TPU:1, one launch (start us, length us, event | category | flops | bytes accessed | tf_op | source)
XLA Modules:
  0.0 63.3 jit_solution(1937357248232060694)
XLA Ops:
  0.6 60.1 %exchange.1 = (bf16[2,16,32,256]{3,2,1,0:T(8,128)(2,1)}, f32[2,96,256]{2,1,0:T(8,128)}, f32[2,96,256]{2,1,0:T(8,128)}) custom-call(bf16[384,6144]{1,0:T(8,128)(2,1)} %m_ref.1, s32[96,96]{1,0:T(8,128)} %pm_hbm.1, bf16[96,512]{1,0:T(8,128)(2,1)} %a_hbm.1, s32[2,96]{1,0:T(2,128)} %bitcast.2, bf16[96,512]{1,0:T(8,128)(2,1)} %b_hbm.1, s32[2,96]{1,0:T(2,128)} %bitcast.3), custom_call_target="tpu_custom_call" | custom-call | tf_op jit(solution)/shard_map/exchange/pallas_call | solution.py:561
  60.7 2.6 %last.1 = (bf16[96,512]{1,0:T(8,128)(2,1)}, bf16[96,512]{1,0:T(8,128)(2,1)}, f32[512,512]{1,0:T(8,128)}) custom-call(bf16[2,16,32,256]{3,2,1,0:T(8,128)(2,1)} %get-tuple-element.6.r_hbm, f32[2,96,256]{2,1,0:T(8,128)} %get-tuple-element.7.b_hbm, f32[2,96,256]{2,1,0:T(8,128)} %get-tuple-element.8.a_hbm), custom_call_target="tpu_custom_call" | custom-call | tf_op jit(solution)/shard_map/last/pallas_call | solution.py:587
